TPU v7x, 32 devices: a whole 2x2x4 slice. The times are simulated.
32 devices in a mesh: seq: 16 (over z, y, x), head: 2 (over core).
Axes of the slice: x: 2, y: 2, z: 4, core: 2. Of those that a mesh axis runs over, the one named last changes fastest.
Arguments:
- query_vec: bfloat16 [16384, 2048], P('seq', 'head'), may hold values from -6 to 6
- key_vec: bfloat16 [16384, 2048], P('seq', 'head'), may hold values from -6 to 6
- value_vec: bfloat16 [16384, 2048], P('seq', 'head'), may hold values from -60 to 60
- cotangent: bfloat16 [16384, 2048], P('seq', 'head'), may hold values from -6 to 6
- norm_gain: float32 [2048], P('head'), may hold values from 0.5 to 1.5
- doc_ids: int32 [16384], P('seq'), may hold values from 0 to 15, never falling along the last dimension, each value on 1 to 4096 neighbouring positions
- lang_ids: int32 [16384], P('seq'), may hold values from 0 to 15
- loss_table: float32 [16], replicated, may hold values from 0.25 to 4
Outputs:
- grad_query: bfloat16 [16384, 2048], P('seq', 'head')
- grad_key: bfloat16 [16384, 2048], P('seq', 'head')
- grad_value: bfloat16 [16384, 2048], P('seq', 'head')
Inputs may be any that keep to these rules, and one draw needn't show every extreme that they name: `doc_ids`: document numbers never fall along the row, each of 0 to 15 occurs, every document has 1 to 4096 tokens and one has exactly 4096.
All inputs are finite; a program needn't handle non-finite values.
Results may differ from a plain program's by a relative error of at most 0.0058.
Values sent between devices are 32-bit elements; how exact they have to be, the bound alone decides.
A program may use at most 128 MiB of HBM per device.

v0:
```python
import jax
import jax.numpy as jnp
from jax import lax
from jax.sharding import PartitionSpec as P

HEAD_DIM = 128
HEADS = 16


EPSILON = 1e-06


def prefix(shard, axis, combine, identity, reverse):
    count, here = (lax.axis_size(axis), lax.axis_index(axis))
    everything = jax.tree.map(lambda part: lax.all_gather(part, axis), shard)
    start = jax.tree.map(
        lambda part, zero: jnp.broadcast_to(jnp.asarray(zero, part.dtype), part.shape),
        shard,
        identity,
    )

    def hop(k, before):
        at = count - 1 - k if reverse else k
        reached = at > here if reverse else at < here
        new = combine(before, jax.tree.map(lambda part: part[at], everything))
        return jax.tree.map(lambda a, b: jnp.where(reached, a, b), new, before)

    return lax.fori_loop(0, count, hop, start)


def combine(earlier, later):
    early_state, early_doc, early_empty = earlier
    late_state, late_doc, late_empty = later
    match = (early_doc == late_doc).astype(jnp.float32)
    skipped = late_empty > 0.5
    merged = jnp.where(skipped, early_state, late_state + match * early_state)
    return (merged, jnp.where(skipped, early_doc, late_doc), early_empty * late_empty)


def carried_state(own_state, own_doc, target_doc, reverse):
    element = (own_state, own_doc, jnp.zeros((), jnp.float32))
    neutral = (
        jnp.zeros_like(own_state),
        jnp.full((), -1.0, jnp.float32),
        jnp.ones((), jnp.float32),
    )
    if reverse:
        total = prefix(element, "seq", combine, neutral, True)
    else:
        total = prefix(element, "seq", combine, neutral, False)
    return jnp.where(total[1] == target_doc, total[0], 0.0)


def local(query_vec, key_vec, value_vec, cotangent, norm_gain, doc_ids, lang_ids, loss_table):
    row_count = query_vec.shape[0]
    col_count = query_vec.shape[1]
    head_count = col_count // HEAD_DIM
    norm_width = HEADS * HEAD_DIM

    def split_heads(tensor):
        return tensor.reshape(row_count, head_count, HEAD_DIM)

    queries = split_heads(query_vec)
    keys_here = split_heads(key_vec)
    values_here = split_heads(value_vec)
    position = jnp.arange(row_count)
    visible = (position[:, None] >= position[None, :]) & (doc_ids[:, None] == doc_ids[None, :])
    first_doc = doc_ids[0]
    last_doc = doc_ids[row_count - 1]
    in_first = (doc_ids == first_doc)[:, None, None]
    in_last = (doc_ids == last_doc)[:, None, None]
    first_float = first_doc.astype(jnp.float32)
    last_float = last_doc.astype(jnp.float32)
    zero_bf = jnp.zeros((), jnp.bfloat16)
    kept_keys = jnp.where(in_last, keys_here, zero_bf)
    own_state = jnp.einsum(
        "the,thf->hef", kept_keys, values_here, preferred_element_type=jnp.float32
    )
    incoming = carried_state(own_state, last_float, first_float, False).astype(jnp.bfloat16)
    raw_scores = jnp.einsum("the,she->hts", queries, keys_here, preferred_element_type=jnp.float32)
    scores = jnp.where(visible[None], raw_scores, 0.0).astype(jnp.bfloat16)
    inner = jnp.einsum("hts,shf->thf", scores, values_here, preferred_element_type=jnp.float32)
    carried = jnp.einsum("the,hef->thf", queries, incoming, preferred_element_type=jnp.float32)
    head_out = (inner + jnp.where(in_first, carried, 0.0)).reshape(row_count, col_count)
    table_hit = lang_ids[:, None] == jnp.arange(loss_table.shape[0], dtype=jnp.int32)[None, :]
    token_weight = jnp.sum(jnp.where(table_hit, loss_table[None, :], 0.0), axis=1)
    upstream = cotangent.astype(jnp.float32) * token_weight[:, None] * norm_gain[None, :]
    squares = jnp.sum(head_out * head_out, axis=1)
    mixed = jnp.sum(upstream * head_out, axis=1)
    squares, mixed = lax.psum((squares, mixed), "head")
    inv_rms = lax.rsqrt(squares / norm_width + EPSILON)
    grad_out = (
        inv_rms[:, None] * upstream - head_out * (inv_rms**3 * mixed / norm_width)[:, None]
    ).astype(jnp.bfloat16)
    grads = split_heads(grad_out)
    kept_queries = jnp.where(in_first, queries, zero_bf)
    own_back = jnp.einsum("the,thf->hef", kept_queries, grads, preferred_element_type=jnp.float32)
    returning = carried_state(own_back, first_float, last_float, True).astype(jnp.bfloat16)
    grad_raw = jnp.einsum("thf,shf->hts", grads, values_here, preferred_element_type=jnp.float32)
    grad_scores = jnp.where(visible[None], grad_raw, 0.0).astype(jnp.bfloat16)
    grad_q = jnp.einsum("hts,she->the", grad_scores, keys_here, preferred_element_type=jnp.float32)
    grad_q = grad_q + jnp.where(
        in_first,
        jnp.einsum("thf,hef->the", grads, incoming, preferred_element_type=jnp.float32),
        0.0,
    )
    grad_k = jnp.einsum("hts,the->she", grad_scores, queries, preferred_element_type=jnp.float32)
    grad_k = grad_k + jnp.where(
        in_last,
        jnp.einsum("shf,hef->she", values_here, returning, preferred_element_type=jnp.float32),
        0.0,
    )
    grad_v = jnp.einsum("hts,thf->shf", scores, grads, preferred_element_type=jnp.float32)
    grad_v = grad_v + jnp.where(
        in_last,
        jnp.einsum("she,hef->shf", keys_here, returning, preferred_element_type=jnp.float32),
        0.0,
    )
    return (
        grad_q.reshape(row_count, col_count).astype(jnp.bfloat16),
        grad_k.reshape(row_count, col_count).astype(jnp.bfloat16),
        grad_v.reshape(row_count, col_count).astype(jnp.bfloat16),
    )


def solution(mesh):
    in_specs = (
        P("seq", "head"),
        P("seq", "head"),
        P("seq", "head"),
        P("seq", "head"),
        P("head"),
        P("seq"),
        P("seq"),
        P(),
    )
    out_specs = (P("seq", "head"), P("seq", "head"), P("seq", "head"))
    return jax.shard_map(local, mesh=mesh, in_specs=in_specs, out_specs=out_specs, check_vma=False)
```

profile of v0, /device:TPU:0, one launch (start us, length us, event | category | flops | bytes accessed | tf_op | source)
XLA Modules:
  0.0 455.3 jit_solution(1919332419831122488)
XLA Ops:
  7.2 1.4 fusion.33
  8.7 3.5 copy.86
  12.2 4.1 copy.60
  17.6 3.2 fusion.8
  22.2 3.9 copy.82
  28.7 44.3 %all-reduce.3 = (f32[16]{0:T(128)S(1)}, f32[16]{0:T(128)S(1)}, f32[16]{0:T(128)S(1)}) all-reduce(f32[16]{0:T(128)S(1)} %dynamic-update-slice, f32[16]{0:T(128)S(1)} %dynamic-update-slice.1, f32[16]{0:T(128)S(1)} %dynamic-update-slice.2), channel_id=1, replica_groups=mesh['seq'=16,'head'=2] {'seq'}, use_global_device_ids=true, to_apply=%add | all-reduce | flops 48 | bytes 384
  73.7 10.8 %select_convert_fusion.1 = bf16[8,1024,1024]{2,1,0:T(8,128)(2,1)} fusion(pred[1024,1024]{1,0:T(8,128)(4,1)S(1)} %fusion.2, bf16[1024,8,128]{0,2,1:T(8,128)(2,1)} %bitcast.103, bf16[1024,1024]{1,0:T(8,128)(2,1)} %param.13), kind=kOutput, calls=%fused_computation.5 | convolution fusion | flops 2164260864 | bytes 22020096 | tf_op jit(solution)/shard_map/the,she->hts/dot_general | solution.py:80
  84.5 12.3 %fusion.3 = f32[8,1024,128]{1,2,0:T(8,128)} fusion(bf16[8,1024,1024]{2,1,0:T(8,128)(2,1)} %select_convert_fusion.1, bf16[1024,1024]{1,0:T(8,128)(2,1)S(1)} %copy-done), kind=kOutput, calls=%fused_computation.18 | convolution fusion | flops 2147483648 | bytes 23068672 | tf_op jit(solution)/shard_map/hts,shf->thf/dot_general | solution.py:82
  96.8 40.2 %all-gather.5.cloned.1.call-done = f32[128,128,128]{2,1,0:T(8,128)} async-done(((f32[8,128,128]{2,1,0:T(8,128)}), f32[128,128,128]{2,1,0:T(8,128)}) %all-gather.5.cloned.1.call-update) | async-done | bytes 8388624 | tf_op jit(solution)/shard_map/all_gather | solution.py:15
  137.0 72.5 %while.34 = (s32[]{:T(128)}, f32[8,128,128]{2,1,0:T(8,128)S(1)}, f32[]{:T(128)}, s32[]{:T(128)}, f32[16]{0:T(128)S(1)}, /*index=5*/f32[16,8,128,128]{3,2,1,0:T(8...) while((s32[]{:T(128)}, f32[8,128,128]{2,1,0:T(8,128)S(1)}, f32[]{:T(128)}, s32[]{:T(128)}, ...), condition=%wide.region_1.2_spmd.clone, body=%wide.region_0.1_spmd.clone.sunk | while | flops 655369 | bytes 1573083 | solution.py:28
  140.1 1.4 select_select_fusion.4
  144.7 1.4 select_select_fusion.4
  149.2 1.4 select_select_fusion.4
  153.7 1.4 select_select_fusion.4
  158.3 1.4 select_select_fusion.4
  162.8 1.4 select_select_fusion.4
  167.3 1.4 select_select_fusion.4
  171.9 1.4 select_select_fusion.4
  176.4 1.4 select_select_fusion.4
  190.0 1.4 select_select_fusion.4
  199.1 1.4 select_select_fusion.4
  208.1 1.4 select_select_fusion.4
  209.5 5.7 %multiply_reduce_fusion.1 = (f32[1024]{0:T(1024)S(1)}, f32[1024,8,128]{0,2,1:T(8,128)}) fusion(bf16[1024,8,128]{0,2,1:T(8,128)(2,1)} %bitcast.104, f32[8,128,128]{2,1,0:T(8,128)S(1)} %get-tuple-element.306, pred[]{:T(512)S(6)} %eq.72, pred[1024]{0:T(1024)(128)(4,1)S(1)} %get-tuple-element.402, f32[8,1024,128]{1,2,0:T(8,128)} %fusion.3), kind=kOutput, calls=%fused_computation.15 | convolution fusion | flops 272759808 | bytes 11015169 | tf_op jit(solution)/shard_map/the,hef->thf/dot_general | solution.py:83
  215.2 5.4 %copy.65 = f32[1024,1024]{1,0:T(8,128)} copy(f32[1024,1024]{0,1:T(8,128)} %bitcast.111) | data formatting | bytes 8388608 | tf_op jit(solution)/shard_map/reshape | solution.py:84
  220.6 3.8 multiply_reduce_fusion
  224.4 2.5 all-reduce.4
  226.9 4.3 subtract_convert_fusion
  231.2 3.9 copy.83
  235.1 3.7 fusion.12
  238.9 10.6 %select_convert_fusion = bf16[8,1024,1024]{2,1,0:T(8,128)(2,1)} fusion(pred[1024,1024]{1,0:T(8,128)(4,1)} %copy-done.5, bf16[1024,8,128]{0,2,1:T(8,128)(2,1)} %bitcast.108, bf16[1024,1024]{1,0:T(8,128)(2,1)S(1)} %copy-done), kind=kOutput, calls=%fused_computation.4 | convolution fusion | flops 2164260864 | bytes 22020096 | tf_op jit(solution)/shard_map/thf,shf->hts/dot_general | solution.py:99
  249.5 9.4 %fusion.34 = f32[8,1024,128]{1,2,0:T(8,128)S(1)} fusion(bf16[8,1024,1024]{2,1,0:T(8,128)(2,1)} %select_convert_fusion, bf16[1024,8,128]{0,2,1:T(8,128)(2,1)S(1)} %copy-done.3), kind=kOutput, calls=%fused_computation.57 | convolution fusion | flops 2147483648 | bytes 23068672 | tf_op jit(solution)/shard_map/hts,she->the/dot_general | solution.py:101
  258.9 2.0 fusion.1
  260.9 3.9 copy.77
  264.9 11.2 %fusion.35 = f32[8,128,1024]{2,1,0:T(8,128)} fusion(bf16[1024,8,128]{0,2,1:T(8,128)(2,1)} %bitcast.109, bf16[8,1024,1024]{2,1,0:T(8,128)(2,1)} %select_convert_fusion.1), kind=kOutput, calls=%fused_computation.58 | convolution fusion | flops 2147483648 | bytes 23068672 | tf_op jit(solution)/shard_map/hts,thf->shf/dot_general | solution.py:113
  276.0 74.0 %all-gather.7.cloned.1.call-done = f32[128,128,128]{2,1,0:T(8,128)} async-done(((f32[8,128,128]{2,1,0:T(8,128)}), f32[128,128,128]{2,1,0:T(8,128)}) %all-gather.7.cloned.1.call-update) | async-done | bytes 8388624 | tf_op jit(solution)/shard_map/all_gather | solution.py:15
  350.1 72.6 %while.35 = (s32[]{:T(128)}, f32[8,128,128]{2,1,0:T(8,128)S(1)}, f32[]{:T(128)}, s32[]{:T(128)}, f32[16]{0:T(128)S(1)}, /*index=5*/f32[16,8,128,128]{3,2,1,0:T(8...) while((s32[]{:T(128)}, f32[8,128,128]{2,1,0:T(8,128)S(1)}, ...), condition=%wide.region_8.9_spmd.clone, body=%wide.region_7.8_spmd.clone.sunk | while | flops 655373 | bytes 1573145 | solution.py:28
  353.2 1.4 select_select_fusion.5
  357.7 1.4 select_select_fusion.5
  371.3 1.4 select_select_fusion.5
  385.0 1.4 select_select_fusion.5
  398.6 1.4 select_select_fusion.5
  412.2 1.4 select_select_fusion.5
  416.7 1.4 select_select_fusion.5
  422.7 2.9 fusion.5
  427.1 2.2 add_convert_fusion
  429.3 3.9 copy.79
  433.2 11.3 %fusion = bf16[1024,8,128]{0,2,1:T(8,128)(2,1)} fusion(f32[8,128,1024]{2,1,0:T(8,128)} %fusion.5, bf16[1024,8,128]{0,2,1:T(8,128)(2,1)} %bitcast.106, bf16[8,1024,1024]{2,1,0:T(8,128)(2,1)} %select_convert_fusion, pred[1024]{0:T(1024)(128)(4,1)S(1)} %get-tuple-element.401), kind=kOutput, calls=%fused_computation.7 | convolution fusion | flops 2150629376 | bytes 25166848 | tf_op jit(solution)/shard_map/hts,the->she/dot_general | solution.py:107
  444.5 3.9 copy.78
  (116 shorter events, 61.7 us)
Async XLA Ops:
  7.2 10.4 %copy-start = (bf16[1024,1024]{1,0:T(8,128)(2,1)S(1)}, bf16[1024,1024]{1,0:T(8,128)(2,1)}, u32[]{:S(2)}) copy-start(bf16[1024,1024]{1,0:T(8,128)(2,1)} %param.14) | copy-start | bytes 6291460
  7.2 129.8 %all-gather.5.cloned.1.call-start = ((), (), s32[]{:S(2)}) async-start(), calls=%async_computation | async-start | bytes 8912896 | tf_op jit(solution)/shard_map/all_gather | solution.py:15
  12.2 4.1 copy-start.6
  20.8 329.3 %all-gather.7.cloned.1.call-start = ((), (), s32[]{:S(2)}) async-start(), calls=%async_computation.1 | async-start | bytes 8912896 | tf_op jit(solution)/shard_map/all_gather | solution.py:15
  22.1 4.0 copy-start.10
  22.2 50.8 %copy-start.8 = (s32[1024]{0:T(1024)S(1)}, s32[1024]{0:T(1024)}, u32[]{:S(2)}) copy-start(s32[1024]{0:T(1024)} %param.18) | copy-start | bytes 12292
  22.2 50.8 %copy-start.9 = (f32[16]{0:T(128)S(1)}, f32[16]{0:T(128)}, u32[]{:S(2)}) copy-start(f32[16]{0:T(128)} %param.19) | copy-start | bytes 196
  73.7 10.8 %copy-start.5 = (pred[1024,1024]{1,0:T(8,128)(4,1)}, pred[1024,1024]{1,0:T(8,128)(4,1)S(1)}, u32[]{:S(2)}) copy-start(pred[1024,1024]{1,0:T(8,128)(4,1)S(1)} %fusion.2) | copy-start | bytes 3145732
  215.2 5.4 %copy-start.7 = (f32[1024]{0:T(1024)S(1)}, f32[1024]{0:T(1024)}, u32[]{:S(2)}) copy-start(f32[1024]{0:T(1024)} %param.16) | copy-start | bytes 12292
  238.9 10.6 %copy-start.3 = (bf16[1024,8,128]{0,2,1:T(8,128)(2,1)S(1)}, bf16[1024,8,128]{0,2,1:T(8,128)(2,1)}, u32[]{:S(2)}) copy-start(bf16[1024,8,128]{0,2,1:T(8,128)(2,1)} %copy.60) | copy-start | bytes 6291460
  249.5 9.4 %copy-start.1 = (bf16[1024,1024]{0,1:T(8,128)(2,1)S(1)}, bf16[1024,1024]{0,1:T(8,128)(2,1)}, u32[]{:S(2)}) copy-start(bf16[1024,1024]{0,1:T(8,128)(2,1)} %copy.83) | copy-start | bytes 6291460
  422.7 3.4 copy-start.2
  422.7 4.4 copy-start.4
Sparse Core Ops, SparseCore 0:
  20.9 116.0 all-gather.4
  239.0 111.0 all-gather.6
where the time goes:
time: 458 us; the launch traced here: 455 us
  waiting for transfers between devices  114 us (25%)
  matrix products  85.2 us (19%)
  local copies, waits for them, and re-layouts  75.9 us (17%)
  loops' own time  63.5 us (14%)
  other arithmetic  54.1 us (12%)
  blocking collectives  46.8 us (10%)
  between operations  15.5 us (3%)
    all_gather x2, waiting for transfers between devices, prefix(): everything = jax.tree.map(lambda part: lax.all_gather(part, axis), shard)  114 us
    another operation x2, loops' own time, prefix(): return lax.fori_loop(0, count, hop, start)  63.5 us
    unnamed x1, blocking collectives  44.3 us
    select_n x32, other arithmetic, hop(): return jax.tree.map(lambda a, b: jnp.where(reached, a, b), new, before)  44 us
    dynamic_slice x64, local copies, waits for them, and re-layouts, hop(): new = combine(before, jax.tree.map(lambda part: part[at], everything))  37.6 us
    unnamed x33, local copies, waits for them, and re-layouts  19.5 us
    dot_general x1, matrix products, local(): jnp.einsum('hts,shf->thf', scores, values_here, preferred_element_type=jn...  12.3 us
    reshape x3, local copies, waits for them, and re-layouts, split_heads(): return tensor.reshape(row_count, head_count, HEAD_DIM)  12 us
  transfers between devices with their start and end apart: 2, of which 2 were waited for; matrix products, arithmetic and copies ran while one was open for 15% of the time, Pallas kernels for 0%

commit v1 on v0

v1 whole, which is shorter than its diff:
```python
import functools

import jax
import jax.numpy as jnp
from jax import lax
from jax.experimental import pallas as pl
from jax.experimental.pallas import tpu as pltpu
from jax.sharding import PartitionSpec as P

HEAD_DIM = 128
HEADS = 16
EPSILON = 1e-06
TILE = 256
LAG_Y = 2
LAG_Z = 4
MESH = pl.DeviceIdType.MESH
F32 = jnp.float32
BF16 = jnp.bfloat16


def dot_nn(a, b):
    return lax.dot_general(a, b, (((1,), (0,)), ((), ())), preferred_element_type=F32)


def dot_nt(a, b):
    return lax.dot_general(a, b, (((1,), (1,)), ((), ())), preferred_element_type=F32)


def dot_tn(a, b):
    return lax.dot_general(a, b, (((0,), (0,)), ((), ())), preferred_element_type=F32)


def same(a, b):
    return jnp.where(a == b, 1.0, 0.0)


def kernel(
    blocks, cores, norm_width,
    table_ref, doc_ref, lang_ref, gain_ref, q_hbm, k_hbm, v_hbm, c_hbm,
    dq_hbm, dk_hbm, dv_hbm,
    q_s, k_s, v_s, c_s, g_s, out_s, dv_s, st_s, mask_s, maskt_s,
    own_s, xin_s, pair_s, yin_s, send_s, zin_s, carry_s, inc_s, ret_s,
    col_s, first_s, last_s, sq_s, mx_s, stat_s, statin_s, meta_s,
    in_sem, out_sem, comm_send, comm_recv, meta_send, meta_recv, stat_send, stat_recv,
):
    heads, rows, _ = q_s.shape
    count = rows // TILE
    here = lax.axis_index("seq")
    core = lax.axis_index("head")
    bit_x = lax.rem(here, 2)
    bit_y = lax.rem(here // 2, 2)
    near = here + 1 - 2 * bit_x
    across = here + 2 - 4 * bit_y
    has_up = here + 4 < blocks
    has_down = here >= 4
    up = jnp.where(has_up, here + 4, here - 4)
    down = jnp.where(has_down, here - 4, here + 4)

    def load(which, h):
        src = (k_hbm, v_hbm, q_hbm, c_hbm)[which]
        dst = (k_s, v_s, q_s, c_s)[which]
        at = pl.ds(pl.multiple_of(h * HEAD_DIM, HEAD_DIM), HEAD_DIM)
        return pltpu.make_async_copy(src.at[:, at], dst.at[h], in_sem.at[which, h])

    def store(which, h):
        src = (c_s, q_s, g_s)[which]
        dst = (dq_hbm, dk_hbm, dv_hbm)[which]
        at = pl.ds(pl.multiple_of(h * HEAD_DIM, HEAD_DIM), HEAD_DIM)
        return pltpu.make_async_copy(src.at[h], dst.at[:, at], out_sem.at[which, h])

    for group in ((0, 1), (2, 3)):
        for h in range(heads):
            for which in group:
                load(which, h).start()

    barrier = pltpu.get_barrier_semaphore()

    def greet(device):
        pl.semaphore_signal(barrier, inc=1, device_id=device, device_id_type=MESH)

    greet((near, core))
    greet((across, core))
    for d in range(1, cores):
        greet((here, lax.rem(core + d, cores)))

    @pl.when(has_up)
    def _():
        greet((up, core))

    @pl.when(has_down)
    def _():
        greet((down, core))

    def remote(src, dst, send_sem, recv_sem, device):
        return pltpu.make_async_remote_copy(
            src_ref=src, dst_ref=dst, send_sem=send_sem, recv_sem=recv_sem,
            device_id=device, device_id_type=MESH,
        )

    def state_copy(back, step, h):
        src = (own_s, pair_s, send_s)[step].at[back, h]
        dst = (xin_s, yin_s, zin_s)[step].at[back, h]
        target = (near, across, down if back else up)[step]
        return remote(
            src, dst, comm_send.at[back, step, h], comm_recv.at[back, step, h], (target, core)
        )

    def meta_copy(step):
        target = (near, across, up, down)[step]
        src = meta_s.at[(0, 2, 4, 4)[step]]
        dst = meta_s.at[(1, 3, 5, 6)[step]]
        return remote(src, dst, meta_send.at[step], meta_recv.at[step], (target, core))

    def stat_copy(d):
        return remote(
            stat_s, statin_s.at[d - 1], stat_send.at[d - 1], stat_recv.at[d - 1],
            (here, lax.rem(core + d, cores)),
        )

    def column(row):
        return jnp.transpose(jnp.broadcast_to(row, (HEAD_DIM, rows)))

    doc_row = doc_ref[...].astype(F32)
    col_s[...] = column(doc_row)
    own_first = col_s[0:1, :]
    own_last = col_s[rows - 1 : rows, :]
    first_s[...] = jnp.where(col_s[...] == own_first, 1.0, 0.0).astype(BF16)
    last_s[...] = jnp.where(col_s[...] == own_last, 1.0, 0.0).astype(BF16)
    meta_s[0, 0:1, :] = own_first
    meta_s[0, 1:2, :] = own_last
    meta_s[0, 2:8, :] = jnp.zeros((6, HEAD_DIM), F32)

    total = 1 + 1 + (cores - 1) + has_up.astype(jnp.int32) + has_down.astype(jnp.int32)
    pl.semaphore_wait(barrier, total)
    meta_copy(0).start()

    @pl.loop(0, heads)
    def _(h):
        load(0, h).wait()
        load(1, h).wait()
        own_s[0, h] = dot_tn(k_s[h] * last_s[...], v_s[h])
        state_copy(0, 0, h).start()

    ahead = lax.broadcasted_iota(jnp.int32, (TILE, HEAD_DIM), 0)
    lane = lax.broadcasted_iota(jnp.int32, (TILE, HEAD_DIM), 1)
    for i in range(count):
        col = col_s[i * TILE : (i + 1) * TILE, :]
        for j in range(rows // HEAD_DIM):
            at = j * HEAD_DIM
            equal = col == doc_row[:, at : at + HEAD_DIM]
            if at < (i + 1) * TILE:
                seen = equal
                if at >= i * TILE:
                    seen = seen & (ahead + i * TILE >= lane + at)
                mask_s[i * TILE : (i + 1) * TILE, at : at + HEAD_DIM] = jnp.where(seen, 1.0, 0.0).astype(BF16)
            if at >= i * TILE:
                seen = equal
                if at < (i + 1) * TILE:
                    seen = seen & (ahead + i * TILE <= lane + at)
                maskt_s[i * TILE : (i + 1) * TILE, at : at + HEAD_DIM] = jnp.where(seen, 1.0, 0.0).astype(BF16)

    lang_row = lang_ref[...]
    weight_row = jnp.zeros((1, rows), F32)
    for i in range(table_ref.shape[0]):
        weight_row = jnp.where(lang_row == i, table_ref[i], weight_row)

    meta_copy(0).wait_recv()
    near_first = meta_s[1, 0:1, :]
    near_last = meta_s[1, 1:2, :]
    pair_first = jnp.where(bit_x == 0, own_first, near_first)
    pair_last = jnp.where(bit_x == 0, near_last, own_last)
    meta_s[2, 0:1, :] = pair_first
    meta_s[2, 1:2, :] = pair_last
    meta_s[2, 2:8, :] = jnp.zeros((6, HEAD_DIM), F32)
    meta_copy(1).start()
    sq_s[...] = jnp.zeros_like(sq_s)
    mx_s[...] = jnp.zeros_like(mx_s)
    meta_copy(1).wait_recv()
    other_first = meta_s[3, 0:1, :]
    other_last = meta_s[3, 1:2, :]
    group_first = jnp.where(bit_y == 0, pair_first, other_first)
    group_last = jnp.where(bit_y == 0, other_last, pair_last)
    meta_s[4, 0:1, :] = group_first
    meta_s[4, 1:2, :] = group_last
    meta_s[4, 2:8, :] = jnp.zeros((6, HEAD_DIM), F32)

    @pl.when(has_up)
    def _():
        meta_copy(2).start()

    @pl.when(has_down)
    def _():
        meta_copy(3).start()

    def factors(x, y, mine, target, theirs, other, group):
        x_on = x.astype(F32)
        y_on = y.astype(F32)
        equal = same(mine, theirs)
        pair = (jnp.where(x == 1, 1.0, equal), jnp.where(x == 1, equal, 1.0))
        take = (x_on * same(theirs, target), y_on * same(other, target))
        send = (same(mine, group), (1.0 - x_on) * same(theirs, group), 1.0 - y_on)
        return pair, take, send

    ahead_w = factors(bit_x, bit_y, own_last, own_first, near_last, other_last, group_last)
    back_w = factors(1 - bit_x, 1 - bit_y, own_first, own_last, near_first, other_first, group_first)

    def step_x(back, h):
        pair = (back_w if back else ahead_w)[0]
        state_copy(back, 0, h).wait_recv()
        pair_s[back, h] = pair[0] * own_s[back, h] + pair[1] * xin_s[back, h]
        state_copy(back, 1, h).start()

    def step_y(back, h):
        take, send = (back_w if back else ahead_w)[1:]
        state_copy(back, 1, h).wait_recv()
        near_state = xin_s[back, h]
        far_state = yin_s[back, h]
        send_s[back, h] = send[0] * own_s[back, h] + send[1] * near_state + send[2] * far_state

        @pl.when(has_down if back else has_up)
        def _():
            state_copy(back, 2, h).start()

        carry_s[back, h] = take[0] * near_state + take[1] * far_state

    def step_z(back, h):
        target = own_last if back else own_first

        @pl.when(has_up if back else has_down)
        def _():
            if back:
                end = meta_s[6, 0:1, :]
            else:
                end = meta_s[5, 1:2, :]
            state_copy(back, 2, h).wait_recv()
            carry_s[back, h] += same(end, target) * zin_s[back, h]

        return carry_s[back, h].astype(BF16)

    @pl.when(has_down)
    def _():
        meta_copy(2).wait_recv()

    @pl.when(has_up)
    def _():
        meta_copy(3).wait_recv()

    @pl.loop(0, heads + LAG_Z)
    def _(t):
        @pl.when(t < heads)
        def _():
            load(2, t).wait()
            load(3, t).wait()
            for i in range(count):
                lo, hi = i * TILE, (i + 1) * TILE
                scores = dot_nt(q_s[t, lo:hi, :], k_s[t, :hi, :]).astype(BF16) * mask_s[lo:hi, :hi]
                out_s[t, lo:hi, :] = dot_nn(scores, v_s[t, :hi, :])
                turned = dot_nt(k_s[t, lo:hi, :], q_s[t, lo:, :]).astype(BF16)
                st_s[t, lo:hi, lo:] = turned * maskt_s[lo:hi, lo:]
            step_x(0, t)

        @pl.when((t >= LAG_Y) & (t < heads + LAG_Y))
        def _():
            step_y(0, t - LAG_Y)

        @pl.when(t >= LAG_Z)
        def _():
            h = t - LAG_Z
            incoming = step_z(0, h)
            inc_s[h] = incoming
            out = out_s[h] + dot_nn(q_s[h] * first_s[...], incoming)
            out_s[h] = out
            sq_s[...] += out * out
            gain = gain_ref[:, pl.ds(pl.multiple_of(h * HEAD_DIM, HEAD_DIM), HEAD_DIM)]
            mx_s[...] += c_s[h].astype(F32) * gain * out

    stat_s[0:1, :] = jnp.sum(jnp.transpose(sq_s[...]), axis=0, keepdims=True)
    stat_s[1:2, :] = jnp.sum(jnp.transpose(mx_s[...]), axis=0, keepdims=True)
    stat_s[2:8, :] = jnp.zeros((6, rows), F32)
    for d in range(1, cores):
        stat_copy(d).start()
    squares = stat_s[0:1, :]
    mixed = stat_s[1:2, :]
    for d in range(1, cores):
        stat_copy(d).wait_recv()
        squares = squares + statin_s[d - 1, 0:1, :]
        mixed = mixed + statin_s[d - 1, 1:2, :]
    inv_rms = lax.rsqrt(squares / norm_width + EPSILON)
    sq_s[...] = column(inv_rms * weight_row)
    mx_s[...] = column(inv_rms * inv_rms * inv_rms * (mixed * weight_row) / norm_width)

    @pl.loop(0, heads)
    def _(h):
        gain = gain_ref[:, pl.ds(pl.multiple_of(h * HEAD_DIM, HEAD_DIM), HEAD_DIM)]
        grad = c_s[h].astype(F32) * gain * sq_s[...] - out_s[h] * mx_s[...]
        grad = grad.astype(BF16)
        g_s[h] = grad
        own_s[1, h] = dot_tn(q_s[h] * first_s[...], grad)
        state_copy(1, 0, h).start()

    @pl.loop(0, heads + LAG_Z)
    def _(t):
        @pl.when(t < heads)
        def _():
            for i in range(count):
                lo, hi = i * TILE, (i + 1) * TILE
                scores = dot_nt(g_s[t, lo:hi, :], v_s[t, :hi, :]).astype(BF16) * mask_s[lo:hi, :hi]
                grad_q = dot_nn(scores, k_s[t, :hi, :])
                grad_q += dot_nt(g_s[t, lo:hi, :] * first_s[lo:hi, :], inc_s[t])
                c_s[t, lo:hi, :] = grad_q.astype(BF16)
                turned = dot_nt(v_s[t, lo:hi, :], g_s[t, lo:, :]).astype(BF16) * maskt_s[lo:hi, lo:]
                out_s[t, lo:hi, :] = dot_nn(turned, q_s[t, lo:, :])
                dv_s[t, lo:hi, :] = dot_nn(st_s[t, lo:hi, lo:], g_s[t, lo:, :])
            store(0, t).start()
            step_x(1, t)

        @pl.when((t >= LAG_Y) & (t < heads + LAG_Y))
        def _():
            step_y(1, t - LAG_Y)

        @pl.when(t >= LAG_Z)
        def _():
            h = t - LAG_Z
            returning = step_z(1, h)
            ret_s[...] = returning
            q_s[h] = (out_s[h] + dot_nt(v_s[h] * last_s[...], ret_s[...])).astype(BF16)
            store(1, h).start()
            g_s[h] = (dv_s[h] + dot_nn(k_s[h] * last_s[...], ret_s[...])).astype(BF16)
            store(2, h).start()

    @pl.loop(0, heads)
    def _(h):
        for which in range(3):
            store(which, h).wait()
        for back in range(2):
            state_copy(back, 0, h).wait_send()
            state_copy(back, 1, h).wait_send()

            @pl.when(has_down if back else has_up)
            def _():
                state_copy(back, 2, h).wait_send()

    meta_copy(0).wait_send()
    meta_copy(1).wait_send()

    @pl.when(has_up)
    def _():
        meta_copy(2).wait_send()

    @pl.when(has_down)
    def _():
        meta_copy(3).wait_send()

    for d in range(1, cores):
        stat_copy(d).wait_send()


def local(blocks, cores, query_vec, key_vec, value_vec, cotangent, norm_gain, doc_ids, lang_ids, loss_table):
    rows, cols = query_vec.shape
    heads = cols // HEAD_DIM
    state = (2, heads, HEAD_DIM, HEAD_DIM)
    per_head = (heads, rows, HEAD_DIM)
    any_spec = pl.BlockSpec(memory_space=pl.ANY)
    vmem_spec = pl.BlockSpec(memory_space=pltpu.VMEM)
    shape = jax.ShapeDtypeStruct((rows, cols), BF16)
    return pl.pallas_call(
        functools.partial(kernel, blocks, cores, HEADS * HEAD_DIM),
        out_shape=(shape, shape, shape),
        in_specs=[pl.BlockSpec(memory_space=pltpu.SMEM)] + [vmem_spec] * 3 + [any_spec] * 4,
        out_specs=(any_spec,) * 3,
        scratch_shapes=[pltpu.VMEM(per_head, BF16)] * 5
        + [pltpu.VMEM(per_head, F32)] * 2
        + [pltpu.VMEM((heads, rows, rows), BF16)]
        + [pltpu.VMEM((rows, rows), BF16)] * 2
        + [pltpu.VMEM(state, F32)] * 7
        + [
            pltpu.VMEM(state[1:], BF16),
            pltpu.VMEM(state[2:], BF16),
            pltpu.VMEM((rows, HEAD_DIM), F32),
            pltpu.VMEM((rows, HEAD_DIM), BF16),
            pltpu.VMEM((rows, HEAD_DIM), BF16),
            pltpu.VMEM((rows, HEAD_DIM), F32),
            pltpu.VMEM((rows, HEAD_DIM), F32),
            pltpu.VMEM((8, rows), F32),
            pltpu.VMEM((max(cores - 1, 1), 8, rows), F32),
            pltpu.VMEM((7, 8, HEAD_DIM), F32),
            pltpu.SemaphoreType.DMA((4, heads)),
            pltpu.SemaphoreType.DMA((3, heads)),
            pltpu.SemaphoreType.DMA((2, 3, heads)),
            pltpu.SemaphoreType.DMA((2, 3, heads)),
            pltpu.SemaphoreType.DMA((4,)),
            pltpu.SemaphoreType.DMA((4,)),
            pltpu.SemaphoreType.DMA((max(cores - 1, 1),)),
            pltpu.SemaphoreType.DMA((max(cores - 1, 1),)),
        ],
        compiler_params=pltpu.CompilerParams(
            collective_id=0, has_side_effects=True, vmem_limit_bytes=58 * 2**20
        ),
    )(
        loss_table,
        doc_ids.reshape(1, rows),
        lang_ids.reshape(1, rows),
        norm_gain.reshape(1, cols),
        query_vec,
        key_vec,
        value_vec,
        cotangent,
    )


def solution(mesh):
    sizes = dict(mesh.shape)
    in_specs = (
        P("seq", "head"),
        P("seq", "head"),
        P("seq", "head"),
        P("seq", "head"),
        P("head"),
        P("seq"),
        P("seq"),
        P(),
    )
    out_specs = (P("seq", "head"), P("seq", "head"), P("seq", "head"))
    body = functools.partial(local, sizes["seq"], sizes["head"])
    return jax.shard_map(body, mesh=mesh, in_specs=in_specs, out_specs=out_specs, check_vma=False)
```

time: 458 us -> 73.2 us (0.16)
  waiting for transfers between devices: 114 us -> 0 us
  matrix products: 85.2 us -> 0 us
  local copies, waits for them, and re-layouts: 75.9 us -> 6.9 us
  Pallas kernels: 0 us -> 65.5 us
  loops' own time: 63.5 us -> 0 us
  other arithmetic: 54.1 us -> 0 us
  blocking collectives: 46.8 us -> 0 us
  between operations: 15.5 us -> 0.65 us
    all_gather x2 -> x0, waiting for transfers between devices: 114 us -> none  [prefix(): everything = jax.tree.map(lambda part: lax.all_gather(part, axis), shard)]
    dot_general x12 -> x0, matrix products: 85.2 us -> none  [the longest x1 12.3 us: local(): jnp.einsum('hts,shf->thf', scores, values_here, preferred_element_type=jn...]
    pallas_call x0 -> x1, Pallas kernels: none -> 65.5 us  [local(): pl.pallas_call(functools.partial(kernel, blocks, cores, HEADS * HEAD_DIM)...]
    another operation x2 -> x0, loops' own time: 63.5 us -> none  [prefix(): return lax.fori_loop(0, count, hop, start)]
    unnamed x1 -> x0, blocking collectives: 44.3 us -> none
    select_n x32 -> x0, other arithmetic: 44 us -> none  [hop(): return jax.tree.map(lambda a, b: jnp.where(reached, a, b), new, before)]
    dynamic_slice x64 -> x0, local copies, waits for them, and re-layouts: 37.6 us -> none  [hop(): new = combine(before, jax.tree.map(lambda part: part[at], everything))]
    reshape x4 -> x0, local copies, waits for them, and re-layouts: 17.4 us -> none  [the longest x3 12 us: split_heads(): return tensor.reshape(row_count, head_count, HEAD_DIM)]
  transfers between devices with their start and end apart: 2 -> 0, of which waited for: 2 -> 0; matrix products, arithmetic and copies ran while one was open for 15% -> 0% of each run, Pallas kernels for 0% -> 0%
where the time goes in v1:
time: 73.2 us; the launch traced here: 73 us
  Pallas kernels  65.5 us (89%)
  local copies, waits for them, and re-layouts  6.9 us (9%)
    pallas_call x1, Pallas kernels, local(): pl.pallas_call(functools.partial(kernel, blocks, cores, HEADS * HEAD_DIM)...  65.5 us
    unnamed x7, local copies, waits for them, and re-layouts  6.9 us

profile of v1, /device:TPU:0, one launch (start us, length us, event | category | flops | bytes accessed | tf_op | source)
XLA Modules:
  0.0 73.0 jit_solution(16375160897322372342)
XLA Ops:
  0.6 65.5 %shard_map.103 = (bf16[1024,1024]{1,0:T(8,128)(2,1)}, bf16[1024,1024]{1,0:T(8,128)(2,1)}, bf16[1024,1024]{1,0:T(8,128)(2,1)}) custom-call(f32[16]{0:T(128)} %table_ref.1, s32[1,1024]{1,0:T(1,128)} %bitcast.3, s32[1,1024]{1,0:T(1,128)} %bitcast.4, f32[1,1024]{1,0:T(1,128)} %bitcast.5, bf16[1024,1024]{1,0:T(8,128)(2,1)} %q_hbm.1, bf16[1024,1024]{1,0:T(8,128)(2,1)} %k_hbm.1, ...), custom_call_target="tpu_custom_call" | custom-call | tf_op jit(solution)/shard_map/pallas_call | solution.py:366
  66.1 0.0 copy-start.1
  66.1 3.2 %copy.14 = bf16[1024,1024]{1,0:T(8,128)(2,1)} copy(bf16[1024,1024]{1,0:T(8,128)(2,1)} %get-tuple-element.6) | data formatting | bytes 4194304
  69.4 0.0 copy-done.1
  69.4 0.0 copy-start
  69.4 1.3 %copy.15 = bf16[1024,1024]{1,0:T(8,128)(2,1)} copy(bf16[1024,1024]{1,0:T(8,128)(2,1)S(1)} %copy-done.1) | data formatting | bytes 4194304
  70.7 1.0 %copy-done = bf16[1024,1024]{1,0:T(8,128)(2,1)S(1)} copy-done((bf16[1024,1024]{1,0:T(8,128)(2,1)S(1)}, bf16[1024,1024]{1,0:T(8,128)(2,1)}, u32[]{:S(2)}) %copy-start) | copy-done | bytes 2097176
  71.7 1.3 %copy.16 = bf16[1024,1024]{1,0:T(8,128)(2,1)} copy(bf16[1024,1024]{1,0:T(8,128)(2,1)S(1)} %copy-done) | data formatting | bytes 4194304
Async XLA Ops:
  66.1 3.2 %copy-start.1 = (bf16[1024,1024]{1,0:T(8,128)(2,1)S(1)}, bf16[1024,1024]{1,0:T(8,128)(2,1)}, u32[]{:S(2)}) copy-start(bf16[1024,1024]{1,0:T(8,128)(2,1)} %get-tuple-element.7) | copy-start | bytes 6291460
  69.4 2.3 %copy-start = (bf16[1024,1024]{1,0:T(8,128)(2,1)S(1)}, bf16[1024,1024]{1,0:T(8,128)(2,1)}, u32[]{:S(2)}) copy-start(bf16[1024,1024]{1,0:T(8,128)(2,1)} %get-tuple-element.8) | copy-start | bytes 6291460

commit v2 on v1

--- a/solution.py
+++ b/solution.py
@@ -13,6 +13,7 @@
 TILE = 256
 LAG_Y = 2
 LAG_Z = 4
+VMEM_BYTES = 44 * 2**20
 MESH = pl.DeviceIdType.MESH
 F32 = jnp.float32
 BF16 = jnp.bfloat16
@@ -39,7 +40,7 @@
     table_ref, doc_ref, lang_ref, gain_ref, q_hbm, k_hbm, v_hbm, c_hbm,
     dq_hbm, dk_hbm, dv_hbm,
     q_s, k_s, v_s, c_s, g_s, out_s, dv_s, st_s, mask_s, maskt_s,
-    own_s, xin_s, pair_s, yin_s, send_s, zin_s, carry_s, inc_s, ret_s,
+    own_s, xin_s, pair_s, yin_s, send_s, zin_s, carry_s, inc_s, enter_s,
     col_s, first_s, last_s, sq_s, mx_s, stat_s, statin_s, meta_s,
     in_sem, out_sem, comm_send, comm_recv, meta_send, meta_recv, stat_send, stat_recv,
 ):
@@ -124,8 +125,12 @@
     col_s[...] = column(doc_row)
     own_first = col_s[0:1, :]
     own_last = col_s[rows - 1 : rows, :]
-    first_s[...] = jnp.where(col_s[...] == own_first, 1.0, 0.0).astype(BF16)
-    last_s[...] = jnp.where(col_s[...] == own_last, 1.0, 0.0).astype(BF16)
+    spans = [slice(i * TILE, (i + 1) * TILE) for i in range(count)]
+    firsts = [col_s[i * TILE : i * TILE + 1, :] for i in range(count)]
+    lasts = [col_s[(i + 1) * TILE - 1 : (i + 1) * TILE, :] for i in range(count)]
+    for i, span in enumerate(spans):
+        first_s[span, :] = same(col_s[span, :], firsts[i]).astype(BF16)
+        last_s[span, :] = same(col_s[span, :], lasts[i]).astype(BF16)
     meta_s[0, 0:1, :] = own_first
     meta_s[0, 1:2, :] = own_last
     meta_s[0, 2:8, :] = jnp.zeros((6, HEAD_DIM), F32)
@@ -138,26 +143,25 @@
     def _(h):
         load(0, h).wait()
         load(1, h).wait()
-        own_s[0, h] = dot_tn(k_s[h] * last_s[...], v_s[h])
+        running = None
+        for i, span in enumerate(spans):
+            state = dot_tn(k_s[h, span, :] * last_s[span, :], v_s[h, span, :])
+            if i > 0:
+                enter_s[0, h, i] = same(lasts[i - 1], firsts[i]) * running
+                state = state + same(lasts[i - 1], lasts[i]) * running
+            running = state
+        own_s[0, h] = running
         state_copy(0, 0, h).start()
 
     ahead = lax.broadcasted_iota(jnp.int32, (TILE, HEAD_DIM), 0)
     lane = lax.broadcasted_iota(jnp.int32, (TILE, HEAD_DIM), 1)
-    for i in range(count):
-        col = col_s[i * TILE : (i + 1) * TILE, :]
-        for j in range(rows // HEAD_DIM):
-            at = j * HEAD_DIM
-            equal = col == doc_row[:, at : at + HEAD_DIM]
-            if at < (i + 1) * TILE:
-                seen = equal
-                if at >= i * TILE:
-                    seen = seen & (ahead + i * TILE >= lane + at)
-                mask_s[i * TILE : (i + 1) * TILE, at : at + HEAD_DIM] = jnp.where(seen, 1.0, 0.0).astype(BF16)
-            if at >= i * TILE:
-                seen = equal
-                if at < (i + 1) * TILE:
-                    seen = seen & (ahead + i * TILE <= lane + at)
-                maskt_s[i * TILE : (i + 1) * TILE, at : at + HEAD_DIM] = jnp.where(seen, 1.0, 0.0).astype(BF16)
+    for i, span in enumerate(spans):
+        col = col_s[span, :]
+        for at in range(0, TILE, HEAD_DIM):
+            start = i * TILE + at
+            equal = col == doc_row[:, start : start + HEAD_DIM]
+            mask_s[span, at : at + HEAD_DIM] = jnp.where(equal & (ahead >= lane + at), 1.0, 0.0).astype(BF16)
+            maskt_s[span, at : at + HEAD_DIM] = jnp.where(equal & (ahead <= lane + at), 1.0, 0.0).astype(BF16)
 
     lang_row = lang_ref[...]
     weight_row = jnp.zeros((1, rows), F32)
@@ -235,7 +239,7 @@
             state_copy(back, 2, h).wait_recv()
             carry_s[back, h] += same(end, target) * zin_s[back, h]
 
-        return carry_s[back, h].astype(BF16)
+        return carry_s[back, h]
 
     @pl.when(has_down)
     def _():
@@ -251,12 +255,11 @@
         def _():
             load(2, t).wait()
             load(3, t).wait()
-            for i in range(count):
-                lo, hi = i * TILE, (i + 1) * TILE
-                scores = dot_nt(q_s[t, lo:hi, :], k_s[t, :hi, :]).astype(BF16) * mask_s[lo:hi, :hi]
-                out_s[t, lo:hi, :] = dot_nn(scores, v_s[t, :hi, :])
-                turned = dot_nt(k_s[t, lo:hi, :], q_s[t, lo:, :]).astype(BF16)
-                st_s[t, lo:hi, lo:] = turned * maskt_s[lo:hi, lo:]
+            for span in spans:
+                scores = dot_nt(q_s[t, span, :], k_s[t, span, :]).astype(BF16) * mask_s[span, :]
+                out_s[t, span, :] = dot_nn(scores, v_s[t, span, :])
+                turned = dot_nt(k_s[t, span, :], q_s[t, span, :]).astype(BF16)
+                st_s[t, span, :] = turned * maskt_s[span, :]
             step_x(0, t)
 
         @pl.when((t >= LAG_Y) & (t < heads + LAG_Y))
@@ -267,12 +270,17 @@
         def _():
             h = t - LAG_Z
             incoming = step_z(0, h)
-            inc_s[h] = incoming
-            out = out_s[h] + dot_nn(q_s[h] * first_s[...], incoming)
-            out_s[h] = out
-            sq_s[...] += out * out
             gain = gain_ref[:, pl.ds(pl.multiple_of(h * HEAD_DIM, HEAD_DIM), HEAD_DIM)]
-            mx_s[...] += c_s[h].astype(F32) * gain * out
+            for i, span in enumerate(spans):
+                state = incoming
+                if i > 0:
+                    state = enter_s[0, h, i] + same(firsts[i], own_first) * incoming
+                state = state.astype(BF16)
+                inc_s[h, i] = state
+                out = out_s[h, span, :] + dot_nn(q_s[h, span, :] * first_s[span, :], state)
+                out_s[h, span, :] = out
+                sq_s[span, :] += out * out
+                mx_s[span, :] += c_s[h, span, :].astype(F32) * gain * out
 
     stat_s[0:1, :] = jnp.sum(jnp.transpose(sq_s[...]), axis=0, keepdims=True)
     stat_s[1:2, :] = jnp.sum(jnp.transpose(mx_s[...]), axis=0, keepdims=True)
@@ -292,25 +300,32 @@
     @pl.loop(0, heads)
     def _(h):
         gain = gain_ref[:, pl.ds(pl.multiple_of(h * HEAD_DIM, HEAD_DIM), HEAD_DIM)]
-        grad = c_s[h].astype(F32) * gain * sq_s[...] - out_s[h] * mx_s[...]
-        grad = grad.astype(BF16)
-        g_s[h] = grad
-        own_s[1, h] = dot_tn(q_s[h] * first_s[...], grad)
+        running = None
+        for i in reversed(range(count)):
+            span = spans[i]
+            grad = c_s[h, span, :].astype(F32) * gain * sq_s[span, :] - out_s[h, span, :] * mx_s[span, :]
+            grad = grad.astype(BF16)
+            g_s[h, span, :] = grad
+            state = dot_tn(q_s[h, span, :] * first_s[span, :], grad)
+            if i < count - 1:
+                enter_s[1, h, i] = same(firsts[i + 1], lasts[i]) * running
+                state = state + same(firsts[i + 1], firsts[i]) * running
+            running = state
+        own_s[1, h] = running
         state_copy(1, 0, h).start()
 
     @pl.loop(0, heads + LAG_Z)
     def _(t):
         @pl.when(t < heads)
         def _():
-            for i in range(count):
-                lo, hi = i * TILE, (i + 1) * TILE
-                scores = dot_nt(g_s[t, lo:hi, :], v_s[t, :hi, :]).astype(BF16) * mask_s[lo:hi, :hi]
-                grad_q = dot_nn(scores, k_s[t, :hi, :])
-                grad_q += dot_nt(g_s[t, lo:hi, :] * first_s[lo:hi, :], inc_s[t])
-                c_s[t, lo:hi, :] = grad_q.astype(BF16)
-                turned = dot_nt(v_s[t, lo:hi, :], g_s[t, lo:, :]).astype(BF16) * maskt_s[lo:hi, lo:]
-                out_s[t, lo:hi, :] = dot_nn(turned, q_s[t, lo:, :])
-                dv_s[t, lo:hi, :] = dot_nn(st_s[t, lo:hi, lo:], g_s[t, lo:, :])
+            for i, span in enumerate(spans):
+                scores = dot_nt(g_s[t, span, :], v_s[t, span, :]).astype(BF16) * mask_s[span, :]
+                grad_q = dot_nn(scores, k_s[t, span, :])
+                grad_q += dot_nt(g_s[t, span, :] * first_s[span, :], inc_s[t, i])
+                c_s[t, span, :] = grad_q.astype(BF16)
+                turned = dot_nt(v_s[t, span, :], g_s[t, span, :]).astype(BF16) * maskt_s[span, :]
+                out_s[t, span, :] = dot_nn(turned, q_s[t, span, :])
+                dv_s[t, span, :] = dot_nn(st_s[t, span, :], g_s[t, span, :])
             store(0, t).start()
             step_x(1, t)
 
@@ -322,10 +337,16 @@
         def _():
             h = t - LAG_Z
             returning = step_z(1, h)
-            ret_s[...] = returning
-            q_s[h] = (out_s[h] + dot_nt(v_s[h] * last_s[...], ret_s[...])).astype(BF16)
+            for i, span in enumerate(spans):
+                state = returning
+                if i < count - 1:
+                    state = enter_s[1, h, i] + same(lasts[i], own_last) * returning
+                state = state.astype(BF16)
+                grad_k = out_s[h, span, :] + dot_nt(v_s[h, span, :] * last_s[span, :], state)
+                q_s[h, span, :] = grad_k.astype(BF16)
+                grad_v = dv_s[h, span, :] + dot_nn(k_s[h, span, :] * last_s[span, :], state)
+                g_s[h, span, :] = grad_v.astype(BF16)
             store(1, h).start()
-            g_s[h] = (dv_s[h] + dot_nn(k_s[h] * last_s[...], ret_s[...])).astype(BF16)
             store(2, h).start()
 
     @pl.loop(0, heads)
@@ -358,24 +379,26 @@
 def local(blocks, cores, query_vec, key_vec, value_vec, cotangent, norm_gain, doc_ids, lang_ids, loss_table):
     rows, cols = query_vec.shape
     heads = cols // HEAD_DIM
+    count = rows // TILE
     state = (2, heads, HEAD_DIM, HEAD_DIM)
     per_head = (heads, rows, HEAD_DIM)
     any_spec = pl.BlockSpec(memory_space=pl.ANY)
+    hbm_spec = pl.BlockSpec(memory_space=pltpu.HBM)
     vmem_spec = pl.BlockSpec(memory_space=pltpu.VMEM)
     shape = jax.ShapeDtypeStruct((rows, cols), BF16)
     return pl.pallas_call(
         functools.partial(kernel, blocks, cores, HEADS * HEAD_DIM),
         out_shape=(shape, shape, shape),
-        in_specs=[pl.BlockSpec(memory_space=pltpu.SMEM)] + [vmem_spec] * 3 + [any_spec] * 4,
+        in_specs=[pl.BlockSpec(memory_space=pltpu.SMEM)] + [vmem_spec] * 3 + [hbm_spec] * 4,
         out_specs=(any_spec,) * 3,
         scratch_shapes=[pltpu.VMEM(per_head, BF16)] * 5
         + [pltpu.VMEM(per_head, F32)] * 2
-        + [pltpu.VMEM((heads, rows, rows), BF16)]
-        + [pltpu.VMEM((rows, rows), BF16)] * 2
+        + [pltpu.VMEM((heads, rows, TILE), BF16)]
+        + [pltpu.VMEM((rows, TILE), BF16)] * 2
         + [pltpu.VMEM(state, F32)] * 7
         + [
-            pltpu.VMEM(state[1:], BF16),
-            pltpu.VMEM(state[2:], BF16),
+            pltpu.VMEM((heads, count) + state[2:], BF16),
+            pltpu.VMEM((2, heads, count) + state[2:], F32),
             pltpu.VMEM((rows, HEAD_DIM), F32),
             pltpu.VMEM((rows, HEAD_DIM), BF16),
             pltpu.VMEM((rows, HEAD_DIM), BF16),
@@ -394,7 +417,7 @@
             pltpu.SemaphoreType.DMA((max(cores - 1, 1),)),
         ],
         compiler_params=pltpu.CompilerParams(
-            collective_id=0, has_side_effects=True, vmem_limit_bytes=58 * 2**20
+            collective_id=0, has_side_effects=True, vmem_limit_bytes=VMEM_BYTES
         ),
     )(
         loss_table,

time: 73.2 us -> 67.5 us (0.922)
  Pallas kernels: 65.5 us -> 58.3 us
  local copies, waits for them, and re-layouts: 6.9 us -> 8.26 us
    pallas_call x1, Pallas kernels: 65.5 us -> 58.3 us  [local(): pl.pallas_call(functools.partial(kernel, blocks, cores, HEADS * HEAD_DIM)...]
    unnamed x7 -> x13, local copies, waits for them, and re-layouts: 6.9 us -> 8.26 us
where the time goes in v2:
time: 67.5 us; the launch traced here: 67.3 us
  Pallas kernels  58.3 us (86%)
  local copies, waits for them, and re-layouts  8.26 us (12%)
    pallas_call x1, Pallas kernels, local(): pl.pallas_call(functools.partial(kernel, blocks, cores, HEADS * HEAD_DIM)...  58.3 us
    unnamed x13, local copies, waits for them, and re-layouts  8.26 us

profile of v2, /device:TPU:0, one launch (start us, length us, event | category | flops | bytes accessed | tf_op | source)
XLA Modules:
  0.0 67.3 jit_solution(1791308773585243137)
XLA Ops:
  0.6 0.0 copy-start
  0.6 1.6 %copy-done = bf16[1024,1024]{1,0:T(8,128)(2,1)S(1)} copy-done((bf16[1024,1024]{1,0:T(8,128)(2,1)S(1)}, bf16[1024,1024]{1,0:T(8,128)(2,1)}, u32[]{:S(2)}) %copy-start) | copy-done | bytes 2097176
  2.2 0.0 copy-start.1
  2.2 0.7 %copy-done.1 = s32[1024]{0:T(1024)S(1)} copy-done((s32[1024]{0:T(1024)S(1)}, s32[1024]{0:T(1024)}, u32[]{:S(2)}) %copy-start.1) | copy-done | bytes 4120
  2.9 0.0 copy-start.2
  2.9 0.7 %copy-done.2 = s32[1024]{0:T(1024)S(1)} copy-done((s32[1024]{0:T(1024)S(1)}, s32[1024]{0:T(1024)}, u32[]{:S(2)}) %copy-start.2) | copy-done | bytes 4120
  3.6 0.0 copy-start.3
  3.6 0.7 %copy-done.3 = f32[1024]{0:T(1024)S(1)} copy-done((f32[1024]{0:T(1024)S(1)}, f32[1024]{0:T(1024)}, u32[]{:S(2)}) %copy-start.3) | copy-done | bytes 4120
  4.3 0.0 copy-start.4
  4.3 0.7 copy-done.4
  4.9 58.3 %shard_map.103 = (bf16[1024,1024]{1,0:T(8,128)(2,1)S(1)}, bf16[1024,1024]{1,0:T(8,128)(2,1)S(1)}, bf16[1024,1024]{1,0:T(8,128)(2,1)S(1)}) custom-call(f32[16]{0:T(128)S(1)} %copy-done.4, s32[1,1024]{1,0:T(1,128)S(1)} %bitcast.3, s32[1,1024]{1,0:T(1,128)S(1)} %bitcast.4, f32[1,1024]{1,0:T(1,128)S(1)} %bitcast.5, bf16[1024,1024]{1,0:T(8,128)(2,1)S(1)} %copy-done, ...), custom_call_target="tpu_custom_call" | custom-call | tf_op jit(solution)/shard_map/pallas_call | solution.py:389
  63.3 1.3 %copy.14 = bf16[1024,1024]{1,0:T(8,128)(2,1)} copy(bf16[1024,1024]{1,0:T(8,128)(2,1)S(1)} %get-tuple-element.6) | data formatting | bytes 4194304
  64.6 1.3 %copy.15 = bf16[1024,1024]{1,0:T(8,128)(2,1)} copy(bf16[1024,1024]{1,0:T(8,128)(2,1)S(1)} %get-tuple-element.7) | data formatting | bytes 4194304
  65.9 1.3 %copy.16 = bf16[1024,1024]{1,0:T(8,128)(2,1)} copy(bf16[1024,1024]{1,0:T(8,128)(2,1)S(1)} %get-tuple-element.8) | data formatting | bytes 4194304
Async XLA Ops:
  0.6 1.6 %copy-start = (bf16[1024,1024]{1,0:T(8,128)(2,1)S(1)}, bf16[1024,1024]{1,0:T(8,128)(2,1)}, u32[]{:S(2)}) copy-start(bf16[1024,1024]{1,0:T(8,128)(2,1)} %q_hbm.1) | copy-start | bytes 6291460
  2.2 0.7 %copy-start.1 = (s32[1024]{0:T(1024)S(1)}, s32[1024]{0:T(1024)}, u32[]{:S(2)}) copy-start(s32[1024]{0:T(1024)} %param.13) | copy-start | bytes 12292
  2.9 0.7 %copy-start.2 = (s32[1024]{0:T(1024)S(1)}, s32[1024]{0:T(1024)}, u32[]{:S(2)}) copy-start(s32[1024]{0:T(1024)} %param.14) | copy-start | bytes 12292
  3.6 0.7 %copy-start.3 = (f32[1024]{0:T(1024)S(1)}, f32[1024]{0:T(1024)}, u32[]{:S(2)}) copy-start(f32[1024]{0:T(1024)} %param.12) | copy-start | bytes 12292
  4.3 0.7 copy-start.4

commit v3 on v2

--- a/solution.py
+++ b/solution.py
@@ -38,11 +38,11 @@
 def kernel(
     blocks, cores, norm_width,
     table_ref, doc_ref, lang_ref, gain_ref, q_hbm, k_hbm, v_hbm, c_hbm,
-    dq_hbm, dk_hbm, dv_hbm,
-    q_s, k_s, v_s, c_s, g_s, out_s, dv_s, st_s, mask_s, maskt_s,
+    dq_ref, dk_ref, dv_ref,
+    q_s, k_s, v_s, c_s, g_s, out_s, part_s, dv_s, st_s, mask_s, maskt_s,
     own_s, xin_s, pair_s, yin_s, send_s, zin_s, carry_s, inc_s, enter_s,
     col_s, first_s, last_s, sq_s, mx_s, stat_s, statin_s, meta_s,
-    in_sem, out_sem, comm_send, comm_recv, meta_send, meta_recv, stat_send, stat_recv,
+    in_sem, comm_send, comm_recv, meta_send, meta_recv, stat_send, stat_recv,
 ):
     heads, rows, _ = q_s.shape
     count = rows // TILE
@@ -63,11 +63,8 @@
         at = pl.ds(pl.multiple_of(h * HEAD_DIM, HEAD_DIM), HEAD_DIM)
         return pltpu.make_async_copy(src.at[:, at], dst.at[h], in_sem.at[which, h])
 
-    def store(which, h):
-        src = (c_s, q_s, g_s)[which]
-        dst = (dq_hbm, dk_hbm, dv_hbm)[which]
-        at = pl.ds(pl.multiple_of(h * HEAD_DIM, HEAD_DIM), HEAD_DIM)
-        return pltpu.make_async_copy(src.at[h], dst.at[:, at], out_sem.at[which, h])
+    def lanes(h):
+        return pl.ds(pl.multiple_of(h * HEAD_DIM, HEAD_DIM), HEAD_DIM)
 
     for group in ((0, 1), (2, 3)):
         for h in range(heads):
@@ -139,10 +136,7 @@
     pl.semaphore_wait(barrier, total)
     meta_copy(0).start()
 
-    @pl.loop(0, heads)
-    def _(h):
-        load(0, h).wait()
-        load(1, h).wait()
+    def own_ahead(h):
         running = None
         for i, span in enumerate(spans):
             state = dot_tn(k_s[h, span, :] * last_s[span, :], v_s[h, span, :])
@@ -151,7 +145,19 @@
                 state = state + same(lasts[i - 1], lasts[i]) * running
             running = state
         own_s[0, h] = running
-        state_copy(0, 0, h).start()
+
+    pair = 2 if heads % 2 == 0 else 1
+
+    @pl.loop(0, heads // pair)
+    def _(step):
+        group = [step * pair + i for i in range(pair)]
+        for h in group:
+            load(0, h).wait()
+            load(1, h).wait()
+        for h in group:
+            own_ahead(h)
+        for h in group:
+            state_copy(0, 0, h).start()
 
     ahead = lax.broadcasted_iota(jnp.int32, (TILE, HEAD_DIM), 0)
     lane = lax.broadcasted_iota(jnp.int32, (TILE, HEAD_DIM), 1)
@@ -239,8 +245,6 @@
             state_copy(back, 2, h).wait_recv()
             carry_s[back, h] += same(end, target) * zin_s[back, h]
 
-        return carry_s[back, h]
-
     @pl.when(has_down)
     def _():
         meta_copy(2).wait_recv()
@@ -249,38 +253,52 @@
     def _():
         meta_copy(3).wait_recv()
 
-    @pl.loop(0, heads + LAG_Z)
-    def _(t):
-        @pl.when(t < heads)
-        def _():
-            load(2, t).wait()
-            load(3, t).wait()
-            for span in spans:
-                scores = dot_nt(q_s[t, span, :], k_s[t, span, :]).astype(BF16) * mask_s[span, :]
-                out_s[t, span, :] = dot_nn(scores, v_s[t, span, :])
-                turned = dot_nt(k_s[t, span, :], q_s[t, span, :]).astype(BF16)
-                st_s[t, span, :] = turned * maskt_s[span, :]
-            step_x(0, t)
-
-        @pl.when((t >= LAG_Y) & (t < heads + LAG_Y))
-        def _():
-            step_y(0, t - LAG_Y)
-
-        @pl.when(t >= LAG_Z)
-        def _():
-            h = t - LAG_Z
-            incoming = step_z(0, h)
-            gain = gain_ref[:, pl.ds(pl.multiple_of(h * HEAD_DIM, HEAD_DIM), HEAD_DIM)]
-            for i, span in enumerate(spans):
-                state = incoming
-                if i > 0:
-                    state = enter_s[0, h, i] + same(firsts[i], own_first) * incoming
-                state = state.astype(BF16)
-                inc_s[h, i] = state
-                out = out_s[h, span, :] + dot_nn(q_s[h, span, :] * first_s[span, :], state)
-                out_s[h, span, :] = out
-                sq_s[span, :] += out * out
-                mx_s[span, :] += c_s[h, span, :].astype(F32) * gain * out
+    def ahead_local(t):
+        for span in spans:
+            scores = dot_nt(q_s[t, span, :], k_s[t, span, :]).astype(BF16) * mask_s[span, :]
+            part_s[t, span, :] = dot_nn(scores, v_s[t, span, :])
+            turned = dot_nt(k_s[t, span, :], q_s[t, span, :]).astype(BF16)
+            st_s[t, span, :] = turned * maskt_s[span, :]
+
+    def ahead_finish(h):
+        incoming = carry_s[0, h]
+        gain = gain_ref[:, lanes(h)]
+        for i, span in enumerate(spans):
+            state = incoming
+            if i > 0:
+                state = enter_s[0, h, i] + same(firsts[i], own_first) * incoming
+            state = state.astype(BF16)
+            inc_s[h, i] = state
+            out = part_s[h, span, :] + dot_nn(q_s[h, span, :] * first_s[span, :], state)
+            out_s[h, span, :] = out
+            sq_s[span, :] += out * out
+            mx_s[span, :] += c_s[h, span, :].astype(F32) * gain * out
+
+    def run(back, local_part, finish):
+        bounds = sorted({0, heads, LAG_Z, heads + LAG_Z})
+        for begin, end in zip(bounds[:-1], bounds[1:]):
+            with_local = end <= heads
+            with_finish = begin >= LAG_Z
+
+            @pl.loop(begin, end)
+            def _(t):
+                if with_local:
+                    if not back:
+                        load(2, t).wait()
+                        load(3, t).wait()
+                    step_x(back, t)
+
+                @pl.when((t >= LAG_Y) & (t < heads + LAG_Y))
+                def _():
+                    step_y(back, t - LAG_Y)
+
+                if with_finish:
+                    step_z(back, t - LAG_Z)
+                    finish(t - LAG_Z)
+                if with_local:
+                    local_part(t)
+
+    run(0, ahead_local, ahead_finish)
 
     stat_s[0:1, :] = jnp.sum(jnp.transpose(sq_s[...]), axis=0, keepdims=True)
     stat_s[1:2, :] = jnp.sum(jnp.transpose(mx_s[...]), axis=0, keepdims=True)
@@ -297,9 +315,8 @@
     sq_s[...] = column(inv_rms * weight_row)
     mx_s[...] = column(inv_rms * inv_rms * inv_rms * (mixed * weight_row) / norm_width)
 
-    @pl.loop(0, heads)
-    def _(h):
-        gain = gain_ref[:, pl.ds(pl.multiple_of(h * HEAD_DIM, HEAD_DIM), HEAD_DIM)]
+    def own_back(h):
+        gain = gain_ref[:, lanes(h)]
         running = None
         for i in reversed(range(count)):
             span = spans[i]
@@ -312,47 +329,41 @@
                 state = state + same(firsts[i + 1], firsts[i]) * running
             running = state
         own_s[1, h] = running
-        state_copy(1, 0, h).start()
-
-    @pl.loop(0, heads + LAG_Z)
-    def _(t):
-        @pl.when(t < heads)
-        def _():
-            for i, span in enumerate(spans):
-                scores = dot_nt(g_s[t, span, :], v_s[t, span, :]).astype(BF16) * mask_s[span, :]
-                grad_q = dot_nn(scores, k_s[t, span, :])
-                grad_q += dot_nt(g_s[t, span, :] * first_s[span, :], inc_s[t, i])
-                c_s[t, span, :] = grad_q.astype(BF16)
-                turned = dot_nt(v_s[t, span, :], g_s[t, span, :]).astype(BF16) * maskt_s[span, :]
-                out_s[t, span, :] = dot_nn(turned, q_s[t, span, :])
-                dv_s[t, span, :] = dot_nn(st_s[t, span, :], g_s[t, span, :])
-            store(0, t).start()
-            step_x(1, t)
-
-        @pl.when((t >= LAG_Y) & (t < heads + LAG_Y))
-        def _():
-            step_y(1, t - LAG_Y)
-
-        @pl.when(t >= LAG_Z)
-        def _():
-            h = t - LAG_Z
-            returning = step_z(1, h)
-            for i, span in enumerate(spans):
-                state = returning
-                if i < count - 1:
-                    state = enter_s[1, h, i] + same(lasts[i], own_last) * returning
-                state = state.astype(BF16)
-                grad_k = out_s[h, span, :] + dot_nt(v_s[h, span, :] * last_s[span, :], state)
-                q_s[h, span, :] = grad_k.astype(BF16)
-                grad_v = dv_s[h, span, :] + dot_nn(k_s[h, span, :] * last_s[span, :], state)
-                g_s[h, span, :] = grad_v.astype(BF16)
-            store(1, h).start()
-            store(2, h).start()
+
+    @pl.loop(0, heads // pair)
+    def _(step):
+        group = [step * pair + i for i in range(pair)]
+        for h in group:
+            own_back(h)
+        for h in group:
+            state_copy(1, 0, h).start()
+
+    def back_local(t):
+        for i, span in enumerate(spans):
+            scores = dot_nt(g_s[t, span, :], v_s[t, span, :]).astype(BF16) * mask_s[span, :]
+            grad_q = dot_nn(scores, k_s[t, span, :])
+            grad_q += dot_nt(g_s[t, span, :] * first_s[span, :], inc_s[t, i])
+            dq_ref[span, lanes(t)] = grad_q.astype(BF16)
+            turned = dot_nt(v_s[t, span, :], g_s[t, span, :]).astype(BF16) * maskt_s[span, :]
+            part_s[t, span, :] = dot_nn(turned, q_s[t, span, :])
+            dv_s[t, span, :] = dot_nn(st_s[t, span, :], g_s[t, span, :])
+
+    def back_finish(h):
+        returning = carry_s[1, h]
+        for i, span in enumerate(spans):
+            state = returning
+            if i < count - 1:
+                state = enter_s[1, h, i] + same(lasts[i], own_last) * returning
+            state = state.astype(BF16)
+            grad_k = part_s[h, span, :] + dot_nt(v_s[h, span, :] * last_s[span, :], state)
+            dk_ref[span, lanes(h)] = grad_k.astype(BF16)
+            grad_v = dv_s[h, span, :] + dot_nn(k_s[h, span, :] * last_s[span, :], state)
+            dv_ref[span, lanes(h)] = grad_v.astype(BF16)
+
+    run(1, back_local, back_finish)
 
     @pl.loop(0, heads)
     def _(h):
-        for which in range(3):
-            store(which, h).wait()
         for back in range(2):
             state_copy(back, 0, h).wait_send()
             state_copy(back, 1, h).wait_send()
@@ -374,6 +385,15 @@
 
     for d in range(1, cores):
         stat_copy(d).wait_send()
+
+
+def write_out(a_ref, b_ref, c_ref, a_out, b_out, c_out, sem):
+    pairs = ((a_ref, a_out), (b_ref, b_out), (c_ref, c_out))
+    copies = [pltpu.make_async_copy(src, dst, sem.at[i]) for i, (src, dst) in enumerate(pairs)]
+    for copy in copies:
+        copy.start()
+    for copy in copies:
+        copy.wait()
 
 
 def local(blocks, cores, query_vec, key_vec, value_vec, cotangent, norm_gain, doc_ids, lang_ids, loss_table):
@@ -385,14 +405,23 @@
     any_spec = pl.BlockSpec(memory_space=pl.ANY)
     hbm_spec = pl.BlockSpec(memory_space=pltpu.HBM)
     vmem_spec = pl.BlockSpec(memory_space=pltpu.VMEM)
-    shape = jax.ShapeDtypeStruct((rows, cols), BF16)
-    return pl.pallas_call(
+    operands = (
+        loss_table,
+        doc_ids.reshape(1, rows),
+        lang_ids.reshape(1, rows),
+        norm_gain.reshape(1, cols),
+        query_vec,
+        key_vec,
+        value_vec,
+        cotangent,
+    )
+    grads = pl.pallas_call(
         functools.partial(kernel, blocks, cores, HEADS * HEAD_DIM),
-        out_shape=(shape, shape, shape),
+        out_shape=(pltpu.VMEM((rows, cols), BF16),) * 3,
         in_specs=[pl.BlockSpec(memory_space=pltpu.SMEM)] + [vmem_spec] * 3 + [hbm_spec] * 4,
-        out_specs=(any_spec,) * 3,
+        out_specs=(vmem_spec,) * 3,
         scratch_shapes=[pltpu.VMEM(per_head, BF16)] * 5
-        + [pltpu.VMEM(per_head, F32)] * 2
+        + [pltpu.VMEM(per_head, F32)] * 3
         + [pltpu.VMEM((heads, rows, TILE), BF16)]
         + [pltpu.VMEM((rows, TILE), BF16)] * 2
         + [pltpu.VMEM(state, F32)] * 7
@@ -408,7 +437,6 @@
             pltpu.VMEM((max(cores - 1, 1), 8, rows), F32),
             pltpu.VMEM((7, 8, HEAD_DIM), F32),
             pltpu.SemaphoreType.DMA((4, heads)),
-            pltpu.SemaphoreType.DMA((3, heads)),
             pltpu.SemaphoreType.DMA((2, 3, heads)),
             pltpu.SemaphoreType.DMA((2, 3, heads)),
             pltpu.SemaphoreType.DMA((4,)),
@@ -420,15 +448,16 @@
             collective_id=0, has_side_effects=True, vmem_limit_bytes=VMEM_BYTES
         ),
     )(
-        loss_table,
-        doc_ids.reshape(1, rows),
-        lang_ids.reshape(1, rows),
-        norm_gain.reshape(1, cols),
-        query_vec,
-        key_vec,
-        value_vec,
-        cotangent,
+        *(pltpu.with_memory_space_constraint(x, pltpu.HBM) for x in operands),
     )
+    shape = jax.ShapeDtypeStruct((rows, cols), BF16)
+    return pl.pallas_call(
+        write_out,
+        out_shape=(shape,) * 3,
+        in_specs=[any_spec] * 3,
+        out_specs=(any_spec,) * 3,
+        scratch_shapes=[pltpu.SemaphoreType.DMA((3,))],
+    )(*grads)
 
 
 def solution(mesh):

time: 67.5 us -> 252 us (3.73)
  Pallas kernels: 58.3 us -> 247 us
  local copies, waits for them, and re-layouts: 8.26 us -> 3.94 us
    pallas_call x0 -> x1, Pallas kernels: none -> 192 us  [local(): pl.pallas_call(write_out, out_shape=(shape,) * 3, in_specs=[any_spec] * 3...]
    unnamed x13 -> x6, local copies, waits for them, and re-layouts: 8.26 us -> 3.94 us
    pallas_call x1, Pallas kernels: 58.3 us -> 55.5 us  [local(): pl.pallas_call(functools.partial(kernel, blocks, cores, HEADS * HEAD_DIM)...]
where the time goes in v3:
time: 252 us
  Pallas kernels  247 us (98%)
  local copies, waits for them, and re-layouts  3.94 us (2%)
    pallas_call x1, Pallas kernels, local(): pl.pallas_call(write_out, out_shape=(shape,) * 3, in_specs=[any_spec] * 3...  192 us
    pallas_call x1, Pallas kernels, local(): pl.pallas_call(functools.partial(kernel, blocks, cores, HEADS * HEAD_DIM)...  55.5 us

profile of v3, /device:TPU:0, one launch (start us, length us, event | category | flops | bytes accessed | tf_op | source)
XLA Modules:
  0.0 251.8 jit_solution(12800932210371487710)
XLA Ops:
  0.6 55.5 %shard_map.103 = (bf16[1024,1024]{1,0:T(8,128)(2,1)S(1)}, bf16[1024,1024]{1,0:T(8,128)(2,1)S(1)}, bf16[1024,1024]{1,0:T(8,128)(2,1)S(1)}) custom-call(f32[16]{0:T(128)} %table_ref.1, s32[1,1024]{1,0:T(1,128)} %bitcast.3, s32[1,1024]{1,0:T(1,128)} %bitcast.4, f32[1,1024]{1,0:T(1,128)} %bitcast.5, bf16[1024,1024]{1,0:T(8,128)(2,1)} %q_hbm.1, ...), custom_call_target="tpu_custom_call" | custom-call | tf_op jit(solution)/shard_map/pallas_call | solution.py:418
  56.1 0.0 copy-start
  56.1 1.3 copy-done
  57.4 0.0 copy-start.1
  57.5 1.3 copy-done.1
  58.8 0.0 copy-start.2
  58.8 1.3 copy-done.2
  60.1 191.7 %shard_map.104 = (bf16[1024,1024]{1,0:T(8,128)(2,1)}, bf16[1024,1024]{1,0:T(8,128)(2,1)}, bf16[1024,1024]{1,0:T(8,128)(2,1)}) custom-call(bf16[1024,1024]{1,0:T(8,128)(2,1)} %copy-done, bf16[1024,1024]{1,0:T(8,128)(2,1)} %copy-done.1, bf16[1024,1024]{1,0:T(8,128)(2,1)} %copy-done.2), custom_call_target="tpu_custom_call" | custom-call | tf_op jit(solution)/shard_map/pallas_call | solution.py:454
Async XLA Ops:
  56.1 1.3 copy-start
  57.4 1.3 copy-start.1
  58.8 1.3 copy-start.2

commit v4 on v3

--- a/solution.py
+++ b/solution.py
@@ -12,7 +12,8 @@
 EPSILON = 1e-06
 TILE = 256
 LAG_Y = 2
-LAG_Z = 4
+PIECES = 4
+LAG_Z = 6
 VMEM_BYTES = 44 * 2**20
 MESH = pl.DeviceIdType.MESH
 F32 = jnp.float32
@@ -388,8 +389,12 @@
 
 
 def write_out(a_ref, b_ref, c_ref, a_out, b_out, c_out, sem):
-    pairs = ((a_ref, a_out), (b_ref, b_out), (c_ref, c_out))
-    copies = [pltpu.make_async_copy(src, dst, sem.at[i]) for i, (src, dst) in enumerate(pairs)]
+    rows = a_ref.shape[0] // PIECES
+    copies = []
+    for i, (src, dst) in enumerate(((a_ref, a_out), (b_ref, b_out), (c_ref, c_out))):
+        for j in range(PIECES):
+            part = slice(j * rows, (j + 1) * rows)
+            copies.append(pltpu.make_async_copy(src.at[part], dst.at[part], sem.at[i * PIECES + j]))
     for copy in copies:
         copy.start()
     for copy in copies:
@@ -454,10 +459,11 @@
     return pl.pallas_call(
         write_out,
         out_shape=(shape,) * 3,
-        in_specs=[any_spec] * 3,
+        in_specs=[vmem_spec] * 3,
         out_specs=(any_spec,) * 3,
-        scratch_shapes=[pltpu.SemaphoreType.DMA((3,))],
-    )(*grads)
+        scratch_shapes=[pltpu.SemaphoreType.DMA((3 * PIECES,))],
+        compiler_params=pltpu.CompilerParams(vmem_limit_bytes=8 * 2**20),
+    )(*(pltpu.with_memory_space_constraint(x, pltpu.VMEM) for x in grads))
 
 
 def solution(mesh):

time: 252 us -> 58 us (0.23)
  Pallas kernels: 247 us -> 57.2 us
  local copies, waits for them, and re-layouts: 3.94 us -> 0 us
    pallas_call x1, Pallas kernels: 192 us -> 2.75 us  [local(): pl.pallas_call(write_out, out_shape=(shape,) * 3, in_specs=[vmem_spec] *...]
    unnamed x6 -> x0, local copies, waits for them, and re-layouts: 3.94 us -> none
where the time goes in v4:
time: 58 us; the launch traced here: 57.9 us
  Pallas kernels  57.2 us (99%)
  between operations  0.64 us (1%)
    pallas_call x1, Pallas kernels, local(): pl.pallas_call(functools.partial(kernel, blocks, cores, HEADS * HEAD_DIM)...  54.5 us
    pallas_call x1, Pallas kernels, local(): pl.pallas_call(write_out, out_shape=(shape,) * 3, in_specs=[vmem_spec] *...  2.75 us

profile of v4, /device:TPU:0, one launch (start us, length us, event | category | flops | bytes accessed | tf_op | source)
XLA Modules:
  0.0 57.9 jit_solution(9485559679121055180)
XLA Ops:
  0.6 54.5 %shard_map.103 = (bf16[1024,1024]{1,0:T(8,128)(2,1)S(1)}, bf16[1024,1024]{1,0:T(8,128)(2,1)S(1)}, bf16[1024,1024]{1,0:T(8,128)(2,1)S(1)}) custom-call(f32[16]{0:T(128)} %table_ref.1, s32[1,1024]{1,0:T(1,128)} %bitcast.3, s32[1,1024]{1,0:T(1,128)} %bitcast.4, f32[1,1024]{1,0:T(1,128)} %bitcast.5, bf16[1024,1024]{1,0:T(8,128)(2,1)} %q_hbm.1, ...), custom_call_target="tpu_custom_call" | custom-call | tf_op jit(solution)/shard_map/pallas_call | solution.py:423
  55.1 2.8 %shard_map.104 = (bf16[1024,1024]{1,0:T(8,128)(2,1)}, bf16[1024,1024]{1,0:T(8,128)(2,1)}, bf16[1024,1024]{1,0:T(8,128)(2,1)}) custom-call(bf16[1024,1024]{1,0:T(8,128)(2,1)S(1)} %get-tuple-element.6.a_ref, bf16[1024,1024]{1,0:T(8,128)(2,1)S(1)} %get-tuple-element.7.b_ref, bf16[1024,1024]{1,0:T(8,128)(2,1)S(1)} %get-tuple-element.8.c_ref), custom_call_target="tpu_custom_call" | custom-call | tf_op jit(solution)/shard_map/pallas_call | solution.py:459

commit v5 on v4

--- a/solution.py
+++ b/solution.py
@@ -11,6 +11,7 @@
 HEADS = 16
 EPSILON = 1e-06
 TILE = 256
+PART = 64
 LAG_Y = 2
 PIECES = 4
 LAG_Z = 6
@@ -38,12 +39,13 @@
 
 def kernel(
     blocks, cores, norm_width,
-    table_ref, doc_ref, lang_ref, gain_ref, q_hbm, k_hbm, v_hbm, c_hbm,
+    table_hbm, doc_hbm, lang_hbm, gain_hbm, q_hbm, k_hbm, v_hbm, c_hbm,
     dq_ref, dk_ref, dv_ref,
+    table_ref, doc_ref, lang_ref, gain_ref,
     q_s, k_s, v_s, c_s, g_s, out_s, part_s, dv_s, st_s, mask_s, maskt_s,
     own_s, xin_s, pair_s, yin_s, send_s, zin_s, carry_s, inc_s, enter_s,
     col_s, first_s, last_s, sq_s, mx_s, stat_s, statin_s, meta_s,
-    in_sem, comm_send, comm_recv, meta_send, meta_recv, stat_send, stat_recv,
+    small_sem, in_sem, comm_send, comm_recv, meta_send, meta_recv, stat_send, stat_recv,
 ):
     heads, rows, _ = q_s.shape
     count = rows // TILE
@@ -67,6 +69,14 @@
     def lanes(h):
         return pl.ds(pl.multiple_of(h * HEAD_DIM, HEAD_DIM), HEAD_DIM)
 
+    small = [
+        pltpu.make_async_copy(src, dst, small_sem.at[i])
+        for i, (src, dst) in enumerate(
+            ((doc_hbm, doc_ref), (lang_hbm, lang_ref), (gain_hbm, gain_ref), (table_hbm, table_ref))
+        )
+    ]
+    for copy in small:
+        copy.start()
     for group in ((0, 1), (2, 3)):
         for h in range(heads):
             for which in group:
@@ -96,13 +106,19 @@
             device_id=device, device_id_type=MESH,
         )
 
-    def state_copy(back, step, h):
-        src = (own_s, pair_s, send_s)[step].at[back, h]
-        dst = (xin_s, yin_s, zin_s)[step].at[back, h]
+    parts = [slice(i * PART, (i + 1) * PART) for i in range(HEAD_DIM // PART)]
+
+    def state_copy(back, step, h, i):
+        src = (own_s, pair_s, send_s)[step].at[back, h, parts[i]]
+        dst = (xin_s, yin_s, zin_s)[step].at[back, h, parts[i]]
         target = (near, across, down if back else up)[step]
         return remote(
-            src, dst, comm_send.at[back, step, h], comm_recv.at[back, step, h], (target, core)
+            src, dst, comm_send.at[back, step, h, i], comm_recv.at[back, step, h, i], (target, core)
         )
+
+    def send_own(back, h):
+        for i in range(len(parts)):
+            state_copy(back, 0, h, i).start()
 
     def meta_copy(step):
         target = (near, across, up, down)[step]
@@ -119,6 +135,7 @@
     def column(row):
         return jnp.transpose(jnp.broadcast_to(row, (HEAD_DIM, rows)))
 
+    small[0].wait()
     doc_row = doc_ref[...].astype(F32)
     col_s[...] = column(doc_row)
     own_first = col_s[0:1, :]
@@ -158,7 +175,7 @@
         for h in group:
             own_ahead(h)
         for h in group:
-            state_copy(0, 0, h).start()
+            send_own(0, h)
 
     ahead = lax.broadcasted_iota(jnp.int32, (TILE, HEAD_DIM), 0)
     lane = lax.broadcasted_iota(jnp.int32, (TILE, HEAD_DIM), 1)
@@ -170,6 +187,8 @@
             mask_s[span, at : at + HEAD_DIM] = jnp.where(equal & (ahead >= lane + at), 1.0, 0.0).astype(BF16)
             maskt_s[span, at : at + HEAD_DIM] = jnp.where(equal & (ahead <= lane + at), 1.0, 0.0).astype(BF16)
 
+    for copy in small[1:]:
+        copy.wait()
     lang_row = lang_ref[...]
     weight_row = jnp.zeros((1, rows), F32)
     for i in range(table_ref.shape[0]):
@@ -217,22 +236,24 @@
 
     def step_x(back, h):
         pair = (back_w if back else ahead_w)[0]
-        state_copy(back, 0, h).wait_recv()
-        pair_s[back, h] = pair[0] * own_s[back, h] + pair[1] * xin_s[back, h]
-        state_copy(back, 1, h).start()
+        for i, part in enumerate(parts):
+            state_copy(back, 0, h, i).wait_recv()
+            pair_s[back, h, part] = pair[0] * own_s[back, h, part] + pair[1] * xin_s[back, h, part]
+            state_copy(back, 1, h, i).start()
 
     def step_y(back, h):
         take, send = (back_w if back else ahead_w)[1:]
-        state_copy(back, 1, h).wait_recv()
-        near_state = xin_s[back, h]
-        far_state = yin_s[back, h]
-        send_s[back, h] = send[0] * own_s[back, h] + send[1] * near_state + send[2] * far_state
-
-        @pl.when(has_down if back else has_up)
-        def _():
-            state_copy(back, 2, h).start()
-
-        carry_s[back, h] = take[0] * near_state + take[1] * far_state
+        for i, part in enumerate(parts):
+            state_copy(back, 1, h, i).wait_recv()
+            near_state = xin_s[back, h, part]
+            far_state = yin_s[back, h, part]
+            send_s[back, h, part] = send[0] * own_s[back, h, part] + send[1] * near_state + send[2] * far_state
+
+            @pl.when(has_down if back else has_up)
+            def _():
+                state_copy(back, 2, h, i).start()
+
+            carry_s[back, h, part] = take[0] * near_state + take[1] * far_state
 
     def step_z(back, h):
         target = own_last if back else own_first
@@ -243,7 +264,8 @@
                 end = meta_s[6, 0:1, :]
             else:
                 end = meta_s[5, 1:2, :]
-            state_copy(back, 2, h).wait_recv()
+            for i in range(len(parts)):
+                state_copy(back, 2, h, i).wait_recv()
             carry_s[back, h] += same(end, target) * zin_s[back, h]
 
     @pl.when(has_down)
@@ -283,15 +305,15 @@
 
             @pl.loop(begin, end)
             def _(t):
+                @pl.when((t >= LAG_Y) & (t < heads + LAG_Y))
+                def _():
+                    step_y(back, t - LAG_Y)
+
                 if with_local:
+                    step_x(back, t)
                     if not back:
                         load(2, t).wait()
                         load(3, t).wait()
-                    step_x(back, t)
-
-                @pl.when((t >= LAG_Y) & (t < heads + LAG_Y))
-                def _():
-                    step_y(back, t - LAG_Y)
 
                 if with_finish:
                     step_z(back, t - LAG_Z)
@@ -337,7 +359,7 @@
         for h in group:
             own_back(h)
         for h in group:
-            state_copy(1, 0, h).start()
+            send_own(1, h)
 
     def back_local(t):
         for i, span in enumerate(spans):
@@ -366,12 +388,14 @@
     @pl.loop(0, heads)
     def _(h):
         for back in range(2):
-            state_copy(back, 0, h).wait_send()
-            state_copy(back, 1, h).wait_send()
+            for i in range(len(parts)):
+                state_copy(back, 0, h, i).wait_send()
+                state_copy(back, 1, h, i).wait_send()
 
             @pl.when(has_down if back else has_up)
             def _():
-                state_copy(back, 2, h).wait_send()
+                for i in range(len(parts)):
+                    state_copy(back, 2, h, i).wait_send()
 
     meta_copy(0).wait_send()
     meta_copy(1).wait_send()
@@ -423,9 +447,15 @@
     grads = pl.pallas_call(
         functools.partial(kernel, blocks, cores, HEADS * HEAD_DIM),
         out_shape=(pltpu.VMEM((rows, cols), BF16),) * 3,
-        in_specs=[pl.BlockSpec(memory_space=pltpu.SMEM)] + [vmem_spec] * 3 + [hbm_spec] * 4,
+        in_specs=[hbm_spec] * 8,
         out_specs=(vmem_spec,) * 3,
-        scratch_shapes=[pltpu.VMEM(per_head, BF16)] * 5
+        scratch_shapes=[
+            pltpu.SMEM(loss_table.shape, F32),
+            pltpu.VMEM((1, rows), jnp.int32),
+            pltpu.VMEM((1, rows), jnp.int32),
+            pltpu.VMEM((1, cols), F32),
+        ]
+        + [pltpu.VMEM(per_head, BF16)] * 5
         + [pltpu.VMEM(per_head, F32)] * 3
         + [pltpu.VMEM((heads, rows, TILE), BF16)]
         + [pltpu.VMEM((rows, TILE), BF16)] * 2
@@ -441,9 +471,10 @@
             pltpu.VMEM((8, rows), F32),
             pltpu.VMEM((max(cores - 1, 1), 8, rows), F32),
             pltpu.VMEM((7, 8, HEAD_DIM), F32),
+            pltpu.SemaphoreType.DMA((4,)),
             pltpu.SemaphoreType.DMA((4, heads)),
-            pltpu.SemaphoreType.DMA((2, 3, heads)),
-            pltpu.SemaphoreType.DMA((2, 3, heads)),
+            pltpu.SemaphoreType.DMA((2, 3, heads, HEAD_DIM // PART)),
+            pltpu.SemaphoreType.DMA((2, 3, heads, HEAD_DIM // PART)),
             pltpu.SemaphoreType.DMA((4,)),
             pltpu.SemaphoreType.DMA((4,)),
             pltpu.SemaphoreType.DMA((max(cores - 1, 1),)),

time: 58 us -> 61.8 us (1.066)
  Pallas kernels: 57.2 us -> 61 us
    pallas_call x1, Pallas kernels: 54.5 us -> 58.2 us  [local(): pl.pallas_call(functools.partial(kernel, blocks, cores, HEADS * HEAD_DIM)...]
where the time goes in v5:
time: 61.8 us; the launch traced here: 61.6 us
  Pallas kernels  61 us (99%)
  between operations  0.64 us (1%)
    pallas_call x1, Pallas kernels, local(): pl.pallas_call(functools.partial(kernel, blocks, cores, HEADS * HEAD_DIM)...  58.2 us
    pallas_call x1, Pallas kernels, local(): pl.pallas_call(write_out, out_shape=(shape,) * 3, in_specs=[vmem_spec] *...  2.75 us

profile of v5, /device:TPU:0, one launch (start us, length us, event | category | flops | bytes accessed | tf_op | source)
XLA Modules:
  0.0 61.6 jit_solution(11316065905559270009)
XLA Ops:
  0.6 58.2 %shard_map.103 = (bf16[1024,1024]{1,0:T(8,128)(2,1)S(1)}, bf16[1024,1024]{1,0:T(8,128)(2,1)S(1)}, bf16[1024,1024]{1,0:T(8,128)(2,1)S(1)}) custom-call(f32[16]{0:T(128)} %table_hbm.1, s32[1,1024]{1,0:T(1,128)} %bitcast.3, s32[1,1024]{1,0:T(1,128)} %bitcast.4, f32[1,1024]{1,0:T(1,128)} %bitcast.5, bf16[1024,1024]{1,0:T(8,128)(2,1)} %q_hbm.1, ...), custom_call_target="tpu_custom_call" | custom-call | tf_op jit(solution)/shard_map/pallas_call | solution.py:447
  58.9 2.8 %shard_map.104 = (bf16[1024,1024]{1,0:T(8,128)(2,1)}, bf16[1024,1024]{1,0:T(8,128)(2,1)}, bf16[1024,1024]{1,0:T(8,128)(2,1)}) custom-call(bf16[1024,1024]{1,0:T(8,128)(2,1)S(1)} %get-tuple-element.6.a_ref, bf16[1024,1024]{1,0:T(8,128)(2,1)S(1)} %get-tuple-element.7.b_ref, bf16[1024,1024]{1,0:T(8,128)(2,1)S(1)} %get-tuple-element.8.c_ref), custom_call_target="tpu_custom_call" | custom-call | tf_op jit(solution)/shard_map/pallas_call | solution.py:490

commit v6 on v5

--- a/solution.py
+++ b/solution.py
@@ -11,10 +11,10 @@
 HEADS = 16
 EPSILON = 1e-06
 TILE = 256
-PART = 64
-LAG_Y = 2
+PART = 128
+LAG_Y = 1
 PIECES = 4
-LAG_Z = 6
+LAG_Z = 3
 VMEM_BYTES = 44 * 2**20
 MESH = pl.DeviceIdType.MESH
 F32 = jnp.float32
@@ -298,28 +298,38 @@
             mx_s[span, :] += c_s[h, span, :].astype(F32) * gain * out
 
     def run(back, local_part, finish):
-        bounds = sorted({0, heads, LAG_Z, heads + LAG_Z})
+        steps = heads // pair
+        bounds = sorted({0, steps, LAG_Z, steps + LAG_Z})
+
+        def group(step):
+            return [step * pair + i for i in range(pair)]
+
         for begin, end in zip(bounds[:-1], bounds[1:]):
-            with_local = end <= heads
+            with_local = end <= steps
             with_finish = begin >= LAG_Z
 
             @pl.loop(begin, end)
             def _(t):
-                @pl.when((t >= LAG_Y) & (t < heads + LAG_Y))
+                if with_local:
+                    for h in group(t):
+                        if not back:
+                            load(2, h).wait()
+                            load(3, h).wait()
+                        step_x(back, h)
+
+                @pl.when((t >= LAG_Y) & (t < steps + LAG_Y))
                 def _():
-                    step_y(back, t - LAG_Y)
-
+                    for h in group(t - LAG_Y):
+                        step_y(back, h)
+
+                if with_finish:
+                    for h in group(t - LAG_Z):
+                        step_z(back, h)
+                    for h in group(t - LAG_Z):
+                        finish(h)
                 if with_local:
-                    step_x(back, t)
-                    if not back:
-                        load(2, t).wait()
-                        load(3, t).wait()
-
-                if with_finish:
-                    step_z(back, t - LAG_Z)
-                    finish(t - LAG_Z)
-                if with_local:
-                    local_part(t)
+                    for h in group(t):
+                        local_part(h)
 
     run(0, ahead_local, ahead_finish)
 

time: 61.8 us -> 60.5 us (0.979)
  Pallas kernels: 61 us -> 59.8 us
    pallas_call x1, Pallas kernels: 58.2 us -> 57 us  [local(): pl.pallas_call(functools.partial(kernel, blocks, cores, HEADS * HEAD_DIM)...]
where the time goes in v6:
time: 60.5 us; the launch traced here: 60.4 us
  Pallas kernels  59.8 us (99%)
  between operations  0.64 us (1%)
    pallas_call x1, Pallas kernels, local(): pl.pallas_call(functools.partial(kernel, blocks, cores, HEADS * HEAD_DIM)...  57 us
    pallas_call x1, Pallas kernels, local(): pl.pallas_call(write_out, out_shape=(shape,) * 3, in_specs=[vmem_spec] *...  2.75 us

profile of v6, /device:TPU:0, one launch (start us, length us, event | category | flops | bytes accessed | tf_op | source)
XLA Modules:
  0.0 60.4 jit_solution(8438400374319769170)
XLA Ops:
  0.6 57.0 %shard_map.103 = (bf16[1024,1024]{1,0:T(8,128)(2,1)S(1)}, bf16[1024,1024]{1,0:T(8,128)(2,1)S(1)}, bf16[1024,1024]{1,0:T(8,128)(2,1)S(1)}) custom-call(f32[16]{0:T(128)} %table_hbm.1, s32[1,1024]{1,0:T(1,128)} %bitcast.3, s32[1,1024]{1,0:T(1,128)} %bitcast.4, f32[1,1024]{1,0:T(1,128)} %bitcast.5, bf16[1024,1024]{1,0:T(8,128)(2,1)} %q_hbm.1, ...), custom_call_target="tpu_custom_call" | custom-call | tf_op jit(solution)/shard_map/pallas_call | solution.py:457
  57.6 2.8 %shard_map.104 = (bf16[1024,1024]{1,0:T(8,128)(2,1)}, bf16[1024,1024]{1,0:T(8,128)(2,1)}, bf16[1024,1024]{1,0:T(8,128)(2,1)}) custom-call(bf16[1024,1024]{1,0:T(8,128)(2,1)S(1)} %get-tuple-element.6.a_ref, bf16[1024,1024]{1,0:T(8,128)(2,1)S(1)} %get-tuple-element.7.b_ref, bf16[1024,1024]{1,0:T(8,128)(2,1)S(1)} %get-tuple-element.8.c_ref), custom_call_target="tpu_custom_call" | custom-call | tf_op jit(solution)/shard_map/pallas_call | solution.py:500
